TPU v7x, 32 devices: a whole 2x2x4 slice. The times are simulated.
32 devices in a mesh: lat: 4 (over x, core), lev: 8 (over z, y).
Axes of the slice: x: 2, y: 2, z: 4, core: 2. Of those that a mesh axis runs over, the one named last changes fastest.
Arguments:
- spectral: float32 [2, 128, 256, 256], P(None, 'lev', 'lat'), may hold values from -6 to 6
- background: bfloat16 [384, 768, 128], P('lat', 'lev'), may hold values from -6 to 6
- columns: int32 [32, 2048], P(('lat', 'lev')), may hold values from 0 to 9215
- counts: int32 [32], P(('lat', 'lev')), may hold values from 1 to 2048, 32768 in all
- radiances: bfloat16 [32, 2048, 512], P(('lat', 'lev')), may hold values from -6 to 6
- used_pairs: int32 [32, 2048], P(('lat', 'lev')), may hold values from 1 to 256
- channel_weight: float32 [512], replicated, may hold values from 0.25 to 4
- weight_in: bfloat16 [128, 1024], replicated, may hold values from -0.5 to 0.5
- weight_mid: bfloat16 [1024, 1024], replicated, may hold values from -0.1875 to 0.1875
- weight_out: bfloat16 [1024, 512], replicated, may hold values from -0.1875 to 0.1875
Outputs:
- spectral_grad: float32 [2, 128, 256, 256], P(None, 'lev', 'lat')
- grid_grad: float32 [384, 768, 128], P('lat', 'lev')
Inputs may be any that keep to these rules, and one draw needn't show every extreme that they name: Entry [o, s] is the column of owner o's slot s inside o's region of 96 x 96 columns, numbered latitude-major; slots at or past counts[o] are unused. The counts sum to 32768, and the largest is exactly 2048. Block [o, s] uses channels 0 to 2 x used_pairs[o, s] - 1.
All inputs are finite; a program needn't handle non-finite values. No bound on the sum of `counts` on one device may be relied on, other than what follows from the above.
Results may differ from a plain program's by a relative error of at most 0.008.
Values may be sent and summed in bfloat16 or wider, within the bound.
A program may use at most 128 MiB of HBM per device.

v0:
```python
import math

import jax
import jax.numpy as jnp
from jax import lax
from jax.sharding import PartitionSpec as P

M = 256
N = 256
NLAT = 384
NLON = 768


RESCALE_TOP = 2.0**60
RESCALE_BY = 2.0 ** (-60)
RESCALE_LOG = 60.0 * math.log(2.0)
HALF_LOG = 0.5 * math.log(0.5)


def shortened(shard):
    return jax.tree.map(lambda a: a.astype(jnp.bfloat16) if a.dtype == jnp.float32 else a, shard)


def legendre_table(orders, lat_total, degree_total):
    m_float = orders.astype(jnp.float32)
    lat_ids = jnp.arange(lat_total, dtype=jnp.float32)
    latitude = (0.5 - (lat_ids + 0.5) / lat_total) * jnp.pi
    sin_lat = jnp.sin(latitude)
    cos_lat = jnp.cos(latitude)
    order_ids = jnp.arange(1, degree_total, dtype=jnp.float32)
    log_steps = 0.5 * jnp.log((2.0 * order_ids + 1.0) / (2.0 * order_ids))
    log_norm = jnp.sum(
        jnp.where(order_ids[None, :] <= m_float[:, None], log_steps[None, :], 0.0), axis=1
    )
    log_start = HALF_LOG + log_norm[:, None] + m_float[:, None] * jnp.log(cos_lat)[None, :]

    def advance(recur_state, degree):
        previous, earlier, shifts = recur_state
        n_float = degree.astype(jnp.float32)
        on_diagonal = (n_float == m_float)[:, None]
        next_diag = (n_float == m_float + 1.0)[:, None]
        beyond = (n_float > m_float + 1.0)[:, None]
        factor_a = jnp.sqrt(
            jnp.maximum(4.0 * n_float * n_float - 1.0, 1.0)
            / jnp.maximum(n_float * n_float - m_float * m_float, 1.0)
        )
        lower = n_float - 1.0
        factor_b = jnp.sqrt(
            jnp.maximum(lower * lower - m_float * m_float, 0.0)
            / jnp.maximum(4.0 * lower * lower - 1.0, 1.0)
        )
        current = jnp.where(
            beyond,
            factor_a[:, None] * (sin_lat[None, :] * previous - factor_b[:, None] * earlier),
            0.0,
        )
        current = jnp.where(
            next_diag, jnp.sqrt(2.0 * m_float + 3.0)[:, None] * sin_lat[None, :] * previous, current
        )
        current = jnp.where(on_diagonal, 1.0, current)
        oversized = jnp.abs(current) > RESCALE_TOP
        current = jnp.where(oversized, current * RESCALE_BY, current)
        previous = jnp.where(oversized, previous * RESCALE_BY, previous)
        shifts = shifts + oversized.astype(jnp.float32)
        values = current * jnp.exp(log_start + shifts * RESCALE_LOG)
        return ((current, previous, shifts), values)

    zeros = jnp.zeros((orders.shape[0], lat_total), jnp.float32)
    _, legendre = lax.scan(
        advance, (zeros, zeros, zeros), jnp.arange(degree_total, dtype=jnp.int32), unroll=8
    )
    return legendre


def wave_table(wave_total, lon_total):
    wave_ids = jnp.arange(wave_total, dtype=jnp.int32)
    lon_ids = jnp.arange(lon_total, dtype=jnp.int32)
    phase = (wave_ids[:, None] * lon_ids[None, :] % lon_total).astype(jnp.float32) * (
        2.0 * math.pi / lon_total
    )
    weights = jnp.where(wave_ids == 0, 1.0, 2.0).astype(jnp.float32) / wave_total
    return jnp.stack([weights[:, None] * jnp.cos(phase), -weights[:, None] * jnp.sin(phase)])


def silu_slope(inputs):
    sigmoid_v = jax.nn.sigmoid(inputs)
    return sigmoid_v * (1.0 + inputs * (1.0 - sigmoid_v))


def radiance_pass(
    profiles, observed, pair_counts, usable, channel_weight, weight_in, weight_mid, weight_out
):
    pre_first = jnp.dot(profiles, weight_in, preferred_element_type=jnp.float32)
    act_first = jax.nn.silu(pre_first).astype(jnp.bfloat16)
    pre_second = jnp.dot(act_first, weight_mid, preferred_element_type=jnp.float32)
    act_second = jax.nn.silu(pre_second).astype(jnp.bfloat16)
    evolved = jnp.dot(act_second, weight_out, preferred_element_type=jnp.float32)
    channel_ids = jnp.arange(weight_out.shape[1], dtype=jnp.float32)
    active = (channel_ids[None, :] < 2.0 * pair_counts[:, None]) & usable[:, None]
    misfit = jnp.where(
        active, channel_weight[None, :] * (evolved - observed.astype(jnp.float32)), 0.0
    ).astype(jnp.bfloat16)
    back_second = (
        jnp.dot(misfit, weight_out.T, preferred_element_type=jnp.float32) * silu_slope(pre_second)
    ).astype(jnp.bfloat16)
    back_first = (
        jnp.dot(back_second, weight_mid.T, preferred_element_type=jnp.float32)
        * silu_slope(pre_first)
    ).astype(jnp.bfloat16)
    return jnp.dot(back_first, weight_in.T, preferred_element_type=jnp.float32).astype(jnp.bfloat16)


def per_device(
    spectral,
    background,
    columns,
    counts,
    radiances,
    used_pairs,
    channel_weight,
    weight_in,
    weight_mid,
    weight_out,
):
    highest = lax.Precision.HIGHEST
    lat_index = lax.axis_index("lat")
    waves_local = spectral.shape[2]
    orders = lat_index * waves_local + jnp.arange(waves_local, dtype=jnp.int32)
    legendre = legendre_table(orders, NLAT, N)
    fourier = jnp.einsum("nmj,clmn->clmj", legendre, spectral, precision=highest)
    fourier = lax.all_to_all(fourier, "lat", split_axis=3, concat_axis=2, tiled=True)
    dft_table = wave_table(M, NLON)
    increment = jnp.einsum("clmj,cmx->jlx", fourier, dft_table, precision=highest)
    increment = lax.all_to_all(increment, "lev", split_axis=2, concat_axis=1, tiled=True)
    increment = jnp.transpose(increment, (0, 2, 1))
    grid_state = (background.astype(jnp.float32) + increment).astype(jnp.bfloat16)
    band_rows = grid_state.shape[0]
    tile_cols = grid_state.shape[1]
    cell_rows = grid_state.reshape(band_rows * tile_cols, grid_state.shape[2])
    local_cols = columns[0]
    profiles = jnp.take(cell_rows, local_cols, axis=0)
    capacity = local_cols.shape[0]
    usable = jnp.arange(capacity, dtype=jnp.int32) < counts[0]
    observed = radiances[0]
    pair_counts = used_pairs[0].astype(jnp.float32)
    block_grad = radiance_pass(
        profiles, observed, pair_counts, usable, channel_weight, weight_in, weight_mid, weight_out
    )
    grid_grad = (
        jnp.zeros(cell_rows.shape, jnp.float32).at[local_cols].add(block_grad.astype(jnp.float32))
    )
    grid_grad = grid_grad.reshape(band_rows, tile_cols, cell_rows.shape[1])
    grad_rows = lax.all_to_all(
        jnp.transpose(grid_grad, (0, 2, 1)).astype(jnp.bfloat16),
        "lev",
        split_axis=1,
        concat_axis=2,
        tiled=True,
    ).astype(jnp.float32)
    coeff_grad = jnp.einsum("jlx,cmx->clmj", grad_rows, dft_table, precision=highest)
    coeff_grad = lax.all_to_all(
        shortened(coeff_grad), "lat", split_axis=2, concat_axis=3, tiled=True
    ).astype(coeff_grad.dtype)
    spectral_grad = jnp.einsum("nmj,clmj->clmn", legendre, coeff_grad, precision=highest)
    return (spectral_grad, grid_grad)


def solution(mesh):
    in_specs = (
        P(None, "lev", "lat", None),
        P("lat", "lev", None),
        P(("lat", "lev"), None),
        P(("lat", "lev")),
        P(("lat", "lev"), None, None),
        P(("lat", "lev"), None),
        P(),
        P(),
        P(),
        P(),
    )
    out_specs = (P(None, "lev", "lat", None), P("lat", "lev", None))
    return jax.shard_map(
        per_device, mesh=mesh, in_specs=in_specs, out_specs=out_specs, check_vma=False
    )
```

profile of v0, /device:TPU:0, one launch (start us, length us, event | category | flops | bytes accessed | tf_op | source)
XLA Modules:
  0.0 811.7 jit_solution(10531595500693987703)
XLA Ops:
  1.0 275.9 %while.23 = (s32[]{:T(128)}, f32[64,384]{1,0:T(8,128)S(1)}, f32[64,384]{1,0:T(8,128)S(1)}, f32[64,384]{1,0:T(8,128)S(1)}, f32[32,8,64,384]{3,2,1,0:T(8,128)}, /*...) while((s32[]{:T(128)}, f32[64,384]{1,0:T(8,128)S(1)}, ...), condition=%wide.region_2.3_spmd.clone.clone.clone.clone, body=%wide.region_1.2_spmd.clone.clone.clone.clone.sunk | while | flops 7554914 | bytes 6179154 | solution.py:69
  279.7 26.8 %fusion.83 = f32[64,384,32]{1,2,0} fusion(f32[64,256,32]{1,2,0:T(8,128)S(1)} %bitcast.203, f32[256,64,384]{2,1,0:T(8,128)} %bitcast.191), kind=kOutput, calls=%fused_computation.178 | convolution fusion | flops 2415919104 | bytes 30408704
  306.6 7.5 copy.99
  314.1 7.0 reshape.669
  321.1 5.0 all-to-all-start
  330.1 33.5 %all-to-all-done = f32[4,1,196608]{2,1,0:T(1,128)} async-done(((f32[4,1,196608]{2,1,0:T(1,128)}), f32[4,1,196608]{2,1,0:T(1,128)}, u32[]{:S(2)}, u32[]{:S(2)}) %all-to-all-start) | async-done | bytes 3145760 | tf_op jit(solution)/shard_map/all_to_all | solution.py:131
  364.1 11.6 %reduce = f32[4,196608]{1,0:T(4,128)} reduce(f32[4,1,196608]{2,1,0:T(1,128)} %all-to-all-done, f32[]{:T(128)} %broadcast.1294), dimensions={1}, to_apply=%all_to_all.52.reduce_sub_computation | reduce | bytes 6291460 | tf_op jit(solution)/shard_map/all_to_all | solution.py:131
  375.8 7.5 reshape.670
  383.2 6.0 copy.122
  389.2 11.7 %convolution_bitcast_fusion = f32[96,16,768]{2,0,1:T(8,128)} fusion(f32[2,16,256,96]{3,2,0,1:T(8,128)} %bitcast.196, f32[1,256,768]{2,1,0:T(8,128)S(1)} %get-tuple-element.444, f32[1,256,768]{2,1,0:T(8,128)} %get-tuple-element.445), kind=kOutput, calls=%fused_computation.201 | convolution fusion | flops 7248150528 | bytes 9437184 | tf_op jit(solution)/shard_map/clmj,cmx->jlx/dot_general | solution.py:133
  401.0 6.3 copy.102
  407.3 7.4 all-to-all-start.1
  415.5 137.2 %all-to-all-done.1 = f32[96,16,768]{0,1,2:T(8,128)} async-done(((f32[96,16,768]{0,1,2:T(8,128)}), f32[96,16,768]{0,1,2:T(8,128)}, u32[]{:S(2)}, u32[]{:S(2)}) %all-to-all-start.1) | async-done | bytes 4718624 | tf_op jit(solution)/shard_map/all_to_all | solution.py:134
  552.7 8.6 %copy.103 = f32[96,16,8,96]{3,1,2,0:T(8,128)} copy(f32[96,16,8,96]{0,1,3,2:T(8,128)} %bitcast.19) | data formatting | bytes 9437184 | tf_op jit(solution)/shard_map/all_to_all | solution.py:134
  561.2 6.1 copy.104
  567.4 5.2 fusion.85
  572.6 7.6 gather_fusion
  581.6 6.7 fusion.89
  588.3 15.4 %multiply_convert_fusion.1 = bf16[2048,1024]{1,0:T(8,128)(2,1)} fusion(f32[2048,1024]{1,0:T(8,128)} %fusion.89, bf16[1024,512]{1,0:T(8,128)(2,1)} %param.21, bf16[1,2048,512]{2,1,0:T(8,128)(2,1)} %param.16, f32[512]{0:T(512)S(1)} %copy-done.7, f32[2048]{0:T(1024)S(1)} %bitcast.207, pred[2048]{0:T(1024)(128)(4,1)S(1)} %iota_compare_fusion.1), kind=kOutput, calls=%fused_computation.181 | convolution fusion | flops 4331667456 | bytes 15740928 | tf_op jit(solution)/shard_map/dot_general | solution.py:104
  603.7 12.3 %fusion.92 = f32[2048,128]{1,0:T(8,128)} fusion(bf16[128,1024]{1,0:T(8,128)(2,1)S(1)} %copy-done.4, f32[2048,1024]{1,0:T(8,128)} %copy-done.1, bf16[2048,1024]{1,0:T(8,128)(2,1)} %multiply_convert_fusion.1, bf16[1024,1024]{1,0:T(8,128)(2,1)S(1)} %copy-done), kind=kOutput, calls=%fused_computation.197 | convolution fusion | flops 4851236864 | bytes 15990784 | tf_op jit(solution)/shard_map/dot_general | solution.py:110
  615.9 14.3 %scatter_custom_fusion = f32[9216,128]{1,0:T(8,128)} fusion(s32[2048]{0:T(1024)S(1)} %bitcast.206, f32[2048,128]{1,0:T(8,128)} %fusion.92, f32[]{:T(128)} %constant.157.clone.1), kind=kCustom, calls=%fused_computation.199 | custom fusion | flops 262144 | bytes 4719104 | tf_op jit(solution)/shard_map/scatter-add | solution.py:150
  630.2 4.2 convert_bitcast_fusion
  634.4 4.9 copy.105
  639.3 74.7 %all_to_all.72 = bf16[96,128,96]{2,0,1:T(8,128)(2,1)S(1)} all-to-all(bf16[96,128,96]{2,0,1:T(8,128)(2,1)} %copy.105), channel_id=1, replica_groups=mesh['lat'=4,'lev'=8] {'lev'}, dimensions={1} | all-to-all | bytes 4718592 | tf_op jit(solution)/shard_map/all_to_all | solution.py:153
  717.7 6.1 reshape.661
  723.8 7.0 fusion.106
  730.8 4.4 copy.108
  735.2 29.3 %all_to_all.73 = bf16[2,16,256,96]{3,1,0,2:T(8,128)(2,1)S(1)} all-to-all(bf16[2,16,256,96]{3,1,0,2:T(8,128)(2,1)} %copy.108), channel_id=1, replica_groups=mesh['lat'=4,'lev'=8] {'lat'}, dimensions={2} | all-to-all | bytes 3145728 | tf_op jit(solution)/shard_map/all_to_all | solution.py:161
  764.4 4.0 copy.110
  768.5 4.3 all_to_all.67
  772.8 34.7 %fusion.101 = f32[2,16,64,256]{3,1,0,2:T(8,128)} fusion(bf16[2,16,64,384]{3,1,0,2:T(8,128)(2,1)} %all_to_all.67, f32[256,64,384,1]{2,1,0,3:T(8,128)} %bitcast.192), kind=kOutput, calls=%fused_computation.208 | convolution fusion | flops 2415919104 | bytes 28835840 | tf_op jit(solution)/shard_map/nmj,clmj->clmn/dot_general | solution.py:164
  807.5 4.1 copy.112
  (1126 shorter events, 126.5 us)
Async XLA Ops:
  0.6 580.9 %copy-start = (bf16[1024,1024]{1,0:T(8,128)(2,1)S(1)}, bf16[1024,1024]{1,0:T(8,128)(2,1)}, u32[]{:S(2)}) copy-start(bf16[1024,1024]{1,0:T(8,128)(2,1)} %param.20) | copy-start | bytes 6291460
  321.1 42.5 %all-to-all-start = ((f32[4,1,196608]{2,1,0:T(1,128)}), f32[4,1,196608]{2,1,0:T(1,128)}, u32[]{:S(2)}, u32[]{:S(2)}) async-start(f32[4,1,196608]{2,1,0:T(1,128)} %reshape.669), calls=%async_computation | async-start | bytes 6291456 | tf_op jit(solution)/shard_map/all_to_all | solution.py:131
  330.1 59.1 %copy-start.2 = (f32[1,256,768]{2,1,0:T(8,128)}, f32[1,256,768]{2,1,0:T(8,128)S(1)}, u32[]{:S(2)}) copy-start(f32[1,256,768]{2,1,0:T(8,128)S(1)} %get-tuple-element.444) | copy-start | bytes 2359300
  407.3 8.1 copy-start.5
  407.3 8.1 %copy-start.6 = (s32[1,2048]{1,0:T(1,128)S(1)}, s32[1,2048]{1,0:T(1,128)}, u32[]{:S(2)}) copy-start(s32[1,2048]{1,0:T(1,128)} %param.17) | copy-start | bytes 24580
  407.3 145.4 %all-to-all-start.1 = ((f32[96,16,768]{0,1,2:T(8,128)}), f32[96,16,768]{0,1,2:T(8,128)}, u32[]{:S(2)}, u32[]{:S(2)}) async-start(f32[96,16,768]{0,1,2:T(8,128)} %copy.102), calls=%async_computation.1 | async-start | bytes 12582912 | tf_op jit(solution)/shard_map/all_to_all | solution.py:134
  572.6 7.6 copy-start.4
  581.5 6.8 copy-start.1
  581.5 6.8 copy-start.7
  717.7 6.1 copy-start.3
where the time goes:
time: 824 us; the launch traced here: 812 us
  waiting for transfers between devices  171 us (21%)
  loops' own time  162 us (20%)
  local copies, waits for them, and re-layouts  144 us (17%)
  matrix products  116 us (14%)
  blocking collectives  104 us (13%)
  other arithmetic  101 us (12%)
  starting transfers between devices  12.4 us (2%)
    another operation x1, loops' own time, legendre_table(): lax.scan(advance, (zeros, zeros, zeros), jnp.arange(degree_total, dtype=j...  162 us
    all_to_all x1, waiting for transfers between devices, per_device(): lax.all_to_all(increment, 'lev', split_axis=2, concat_axis=1, tiled=True)  137 us
    all_to_all x1, blocking collectives, per_device(): lax.all_to_all(jnp.transpose(grid_grad, (0, 2, 1)).astype(jnp.bfloat16),...  74.7 us
    while x224, other arithmetic  45.5 us
    dot_general x1, matrix products, per_device(): jnp.einsum('nmj,clmj->clmn', legendre, coeff_grad, precision=highest)  34.7 us
    all_to_all x1, waiting for transfers between devices, per_device(): lax.all_to_all(fourier, 'lat', split_axis=3, concat_axis=2, tiled=True)  33.5 us
    dynamic_update_slice x32, local copies, waits for them, and re-layouts, legendre_table(): lax.scan(advance, (zeros, zeros, zeros), jnp.arange(degree_total, dtype=j...  31 us
    all_to_all x1, blocking collectives, per_device(): lax.all_to_all(shortened(coeff_grad), 'lat', split_axis=2, concat_axis=3,...  29.3 us
  transfers between devices with their start and end apart: 2, of which 2 were waited for; matrix products, arithmetic and copies ran while one was open for 0% of the time, Pallas kernels for 0%

commit v1 on v0

v1 whole, which is shorter than its diff:
```python
import functools
import math

import jax
import jax.numpy as jnp
from jax import lax
from jax.experimental import pallas as pl
from jax.experimental.pallas import tpu as pltpu
from jax.sharding import PartitionSpec as P

M = 256
N = 256
NLAT = 384
NLON = 768


RESCALE_BY = 2.0 ** (-60)
RESCALE_LOG = 60.0 * math.log(2.0)
HALF_LOG = 0.5 * math.log(0.5)


CHUNK = 8
GROUP = 16
HALF = 128
SCALE_TOP = 2.0**20


def recurrence_inputs(orders, lat_total, degree_total):
    m_float = orders.astype(jnp.float32)
    half_lats = lat_total // 2
    lat_ids = jnp.arange(half_lats, dtype=jnp.float32)
    latitude = (0.5 - (lat_ids + 0.5) / lat_total) * jnp.pi
    order_ids = jnp.arange(1, degree_total, dtype=jnp.float32)
    log_steps = 0.5 * jnp.log((2.0 * order_ids + 1.0) / (2.0 * order_ids))
    log_norm = jnp.sum(
        jnp.where(order_ids[None, :] <= m_float[:, None], log_steps[None, :], 0.0), axis=1
    )
    log_cos = jnp.log(jnp.cos(latitude))
    log_start = HALF_LOG + log_norm[:, None] + m_float[:, None] * log_cos[None, :]
    pad = 2 * HALF - half_lats
    log_start = jnp.pad(log_start, ((0, 0), (0, pad)))
    sin_lat = jnp.pad(jnp.sin(latitude), (0, pad))[None, :]
    valid = jnp.pad(jnp.ones((half_lats,), jnp.float32), (0, pad))[None, :]
    n_float = jnp.arange(degree_total, dtype=jnp.float32)[None, :]
    m_col = m_float[:, None]
    factor_a = jnp.sqrt(
        jnp.maximum(4.0 * n_float * n_float - 1.0, 1.0)
        / jnp.maximum(n_float * n_float - m_col * m_col, 1.0)
    )
    lower = n_float - 1.0
    factor_b = jnp.sqrt(
        jnp.maximum(lower * lower - m_col * m_col, 0.0)
        / jnp.maximum(4.0 * lower * lower - 1.0, 1.0)
    )

    def chunks(factor):
        folded = factor.reshape(factor.shape[0], degree_total // CHUNK, CHUNK)
        return jnp.transpose(folded, (1, 0, 2))

    return chunks(factor_a), chunks(factor_a * factor_b), log_start, sin_lat, valid


def reversal(size, count):
    rows = lax.broadcasted_iota(jnp.int32, (size, size), 0)
    cols = lax.broadcasted_iota(jnp.int32, (size, size), 1)
    return jnp.where(rows + cols == count - 1, 1.0, 0.0).astype(jnp.bfloat16)


def synthesis_kernel(
    half_lats, fa_ref, fb_ref, log_ref, sin_ref, valid_ref, ord_ref, spec_ref,
    table_ref, four_ref, held
):
    steps = fa_ref.shape[0]
    degrees = steps * CHUNK
    lanes = 2 * HALF
    sin_lat = jnp.broadcast_to(sin_ref[...], (GROUP, lanes))
    valid = jnp.broadcast_to(valid_ref[...], (GROUP, lanes))
    order = ord_ref[...]
    log_start = log_ref[...]

    def step(chunk, state):
        previous, earlier, shifts = state
        scale = jnp.exp(log_start + shifts * RESCALE_LOG) * valid
        col_a = fa_ref[chunk]
        col_b = fb_ref[chunk]
        for k in range(CHUNK):
            degree = chunk * CHUNK + k
            current = (col_a[:, k : k + 1] * sin_lat) * previous - col_b[:, k : k + 1] * earlier
            current = jnp.where(order == degree, 1.0, current)
            values = current * scale
            at = pl.multiple_of(degree * GROUP, GROUP)
            held[0, pl.ds(at, GROUP), :] = values[:, :HALF]
            held[1, pl.ds(at, GROUP), :] = values[:, HALF:]
            earlier, previous = previous, current
        oversized = jnp.maximum(jnp.abs(previous), jnp.abs(earlier)) > SCALE_TOP
        factor = jnp.where(oversized, RESCALE_BY, 1.0)
        return previous * factor, earlier * factor, shifts + jnp.where(oversized, 1.0, 0.0)

    zeros = jnp.zeros((GROUP, lanes), jnp.float32)
    lax.fori_loop(0, steps, step, (zeros, zeros, zeros))

    bands = four_ref.shape[0]
    band = half_lats * 2 // bands
    flip = reversal(lanes, half_lats)
    parity = lax.broadcasted_iota(jnp.int32, spec_ref.shape[1:], 1) % 2
    count = spec_ref.shape[1]
    for m in range(GROUP):
        rows = pl.ds(m, degrees, stride=GROUP)
        table = jnp.concatenate(
            [held[0, rows, :].astype(jnp.bfloat16), held[1, rows, :].astype(jnp.bfloat16)], axis=1
        )
        table_ref[m] = table
        coeffs = spec_ref[m].astype(jnp.float32)
        even = jnp.where(parity == 0, coeffs, 0.0)
        both = jnp.concatenate([even, coeffs - even], axis=0).astype(jnp.bfloat16)
        sums = jnp.dot(both, table, preferred_element_type=jnp.float32)
        north = sums[:count] + sums[count:]
        south = sums[:count] - sums[count:]
        if m % 2:
            south = -south
        south = jnp.dot(south.astype(jnp.bfloat16), flip, preferred_element_type=jnp.float32)
        for b in range(bands // 2):
            four_ref[b, m] = north[:, b * band : (b + 1) * band].astype(jnp.bfloat16)
            four_ref[bands // 2 + b, m] = south[:, b * band : (b + 1) * band].astype(jnp.bfloat16)


def analysis_kernel(half_lats, coeff_ref, table_ref, out_ref):
    bands, group, count, band = coeff_ref.shape
    lanes = 2 * HALF
    flip = reversal(lanes, half_lats)
    parity = lax.broadcasted_iota(jnp.int32, out_ref.shape[1:], 1) % 2
    fill = jnp.zeros((count, lanes - half_lats), jnp.float32)
    for m in range(group):
        bits = [coeff_ref[b, m].astype(jnp.float32) for b in range(bands)]
        north = jnp.concatenate(bits[: bands // 2] + [fill], axis=1)
        south = jnp.concatenate(bits[bands // 2 :] + [fill], axis=1).astype(jnp.bfloat16)
        south = jnp.dot(south, flip, preferred_element_type=jnp.float32)
        if m % 2:
            south = -south
        both = jnp.concatenate([north + south, north - south], axis=0).astype(jnp.bfloat16)
        sums = lax.dot_general(
            both, table_ref[m], (((1,), (1,)), ((), ())), preferred_element_type=jnp.float32
        )
        out_ref[m] = jnp.where(parity == 0, sums[:count], sums[count:])


def synthesis(spectral, orders, lat_total, bands):
    parts, levels, waves, degrees = spectral.shape
    half_lats = lat_total // 2
    count = parts * levels
    lanes = 2 * HALF
    fa, fb, log_start, sin_lat, valid = recurrence_inputs(orders, lat_total, degrees)
    order = jnp.broadcast_to(orders[:, None], (waves, lanes))
    coeffs = jnp.transpose(spectral.astype(jnp.bfloat16), (2, 0, 1, 3)).reshape(
        waves, count, degrees
    )
    band = lat_total // bands
    factor_spec = pl.BlockSpec((degrees // CHUNK, GROUP, CHUNK), lambda g: (0, g, 0))
    wide_spec = pl.BlockSpec((GROUP, lanes), lambda g: (g, 0))
    row_spec = pl.BlockSpec((1, lanes), lambda g: (0, 0))
    return pl.pallas_call(
        functools.partial(synthesis_kernel, half_lats),
        grid=(waves // GROUP,),
        in_specs=[
            factor_spec,
            factor_spec,
            wide_spec,
            row_spec,
            row_spec,
            wide_spec,
            pl.BlockSpec((GROUP, count, degrees), lambda g: (g, 0, 0)),
        ],
        out_specs=[
            pl.BlockSpec((GROUP, degrees, lanes), lambda g: (g, 0, 0)),
            pl.BlockSpec((bands, GROUP, count, band), lambda g: (0, g, 0, 0)),
        ],
        out_shape=[
            jax.ShapeDtypeStruct((waves, degrees, lanes), jnp.bfloat16),
            jax.ShapeDtypeStruct((bands, waves, count, band), jnp.bfloat16),
        ],
        scratch_shapes=[pltpu.VMEM((2, degrees * GROUP, HALF), jnp.float32)],
        compiler_params=pltpu.CompilerParams(vmem_limit_bytes=40 << 20),
    )(fa, fb, log_start, sin_lat, valid, order, coeffs)


def analysis(coeffs, table, lat_total):
    bands, waves, count, band = coeffs.shape
    degrees, lanes = table.shape[1:]
    group = 8
    return pl.pallas_call(
        functools.partial(analysis_kernel, lat_total // 2),
        grid=(waves // group,),
        in_specs=[
            pl.BlockSpec((bands, group, count, band), lambda g: (0, g, 0, 0)),
            pl.BlockSpec((group, degrees, lanes), lambda g: (g, 0, 0)),
        ],
        out_specs=pl.BlockSpec((group, count, degrees), lambda g: (g, 0, 0)),
        out_shape=jax.ShapeDtypeStruct((waves, count, degrees), jnp.float32),
        compiler_params=pltpu.CompilerParams(vmem_limit_bytes=40 << 20),
    )(coeffs, table)


def wave_table(wave_total, lon_total):
    wave_ids = jnp.arange(wave_total, dtype=jnp.int32)
    lon_ids = jnp.arange(lon_total, dtype=jnp.int32)
    phase = (wave_ids[:, None] * lon_ids[None, :] % lon_total).astype(jnp.float32) * (
        2.0 * math.pi / lon_total
    )
    weights = jnp.where(wave_ids == 0, 1.0, 2.0).astype(jnp.float32) / wave_total
    return jnp.stack([weights[:, None] * jnp.cos(phase), -weights[:, None] * jnp.sin(phase)])


def silu_slope(inputs):
    sigmoid_v = jax.nn.sigmoid(inputs)
    return sigmoid_v * (1.0 + inputs * (1.0 - sigmoid_v))


def radiance_pass(
    profiles, observed, pair_counts, usable, channel_weight, weight_in, weight_mid, weight_out
):
    pre_first = jnp.dot(profiles, weight_in, preferred_element_type=jnp.float32)
    act_first = jax.nn.silu(pre_first).astype(jnp.bfloat16)
    pre_second = jnp.dot(act_first, weight_mid, preferred_element_type=jnp.float32)
    act_second = jax.nn.silu(pre_second).astype(jnp.bfloat16)
    evolved = jnp.dot(act_second, weight_out, preferred_element_type=jnp.float32)
    channel_ids = jnp.arange(weight_out.shape[1], dtype=jnp.float32)
    active = (channel_ids[None, :] < 2.0 * pair_counts[:, None]) & usable[:, None]
    misfit = jnp.where(
        active, channel_weight[None, :] * (evolved - observed.astype(jnp.float32)), 0.0
    ).astype(jnp.bfloat16)
    back_second = (
        jnp.dot(misfit, weight_out.T, preferred_element_type=jnp.float32) * silu_slope(pre_second)
    ).astype(jnp.bfloat16)
    back_first = (
        jnp.dot(back_second, weight_mid.T, preferred_element_type=jnp.float32)
        * silu_slope(pre_first)
    ).astype(jnp.bfloat16)
    return jnp.dot(back_first, weight_in.T, preferred_element_type=jnp.float32).astype(jnp.bfloat16)


def per_device(
    spectral,
    background,
    columns,
    counts,
    radiances,
    used_pairs,
    channel_weight,
    weight_in,
    weight_mid,
    weight_out,
):
    lat_index = lax.axis_index("lat")
    parts, levels, waves_local, degrees = spectral.shape
    bands = M // waves_local
    orders = lat_index * waves_local + jnp.arange(waves_local, dtype=jnp.int32)
    table, fourier = synthesis(spectral, orders, NLAT, bands)
    fourier = lax.all_to_all(fourier, "lat", split_axis=0, concat_axis=0, tiled=True)
    band = fourier.shape[3]
    fourier = fourier.reshape(M, parts, levels, band)
    dft_table = wave_table(M, NLON).astype(jnp.bfloat16)
    increment = jnp.einsum(
        "mclj,cmx->jlx", fourier, dft_table, preferred_element_type=jnp.float32
    ).astype(jnp.bfloat16)
    increment = lax.all_to_all(increment, "lev", split_axis=2, concat_axis=1, tiled=True)
    increment = jnp.transpose(increment, (0, 2, 1)).astype(jnp.float32)
    grid_state = (background.astype(jnp.float32) + increment).astype(jnp.bfloat16)
    band_rows = grid_state.shape[0]
    tile_cols = grid_state.shape[1]
    cell_rows = grid_state.reshape(band_rows * tile_cols, grid_state.shape[2])
    local_cols = columns[0]
    profiles = jnp.take(cell_rows, local_cols, axis=0)
    capacity = local_cols.shape[0]
    usable = jnp.arange(capacity, dtype=jnp.int32) < counts[0]
    observed = radiances[0]
    pair_counts = used_pairs[0].astype(jnp.float32)
    block_grad = radiance_pass(
        profiles, observed, pair_counts, usable, channel_weight, weight_in, weight_mid, weight_out
    )
    grid_grad = (
        jnp.zeros(cell_rows.shape, jnp.float32).at[local_cols].add(block_grad.astype(jnp.float32))
    )
    grid_grad = grid_grad.reshape(band_rows, tile_cols, cell_rows.shape[1])
    grad_rows = lax.all_to_all(
        jnp.transpose(grid_grad, (0, 2, 1)).astype(jnp.bfloat16),
        "lev",
        split_axis=1,
        concat_axis=2,
        tiled=True,
    )
    coeff_grad = jnp.einsum(
        "jlx,cmx->mclj", grad_rows, dft_table, preferred_element_type=jnp.float32
    ).astype(jnp.bfloat16)
    coeff_grad = coeff_grad.reshape(bands, waves_local, parts * levels, band)
    coeff_grad = lax.all_to_all(coeff_grad, "lat", split_axis=0, concat_axis=0, tiled=True)
    spectral_grad = analysis(coeff_grad, table, NLAT)
    spectral_grad = jnp.transpose(
        spectral_grad.reshape(waves_local, parts, levels, degrees), (1, 2, 0, 3)
    )
    return (spectral_grad, grid_grad)


def solution(mesh):
    in_specs = (
        P(None, "lev", "lat", None),
        P("lat", "lev", None),
        P(("lat", "lev"), None),
        P(("lat", "lev")),
        P(("lat", "lev"), None, None),
        P(("lat", "lev"), None),
        P(),
        P(),
        P(),
        P(),
    )
    out_specs = (P(None, "lev", "lat", None), P("lat", "lev", None))
    return jax.shard_map(
        per_device, mesh=mesh, in_specs=in_specs, out_specs=out_specs, check_vma=False
    )
```

time: 824 us -> 378 us (0.46); the launches traced: 812 us -> 377 us
  loops' own time: 162 us -> 0 us
  local copies, waits for them, and re-layouts: 144 us -> 57 us
  waiting for transfers between devices: 171 us -> 92.8 us
  other arithmetic: 101 us -> 30.2 us
  matrix products: 116 us -> 45.5 us
  Pallas kernels: 0 us -> 34.7 us
    another operation x1 -> x0, loops' own time: 162 us -> none  [legendre_table(): lax.scan(advance, (zeros, zeros, zeros), jnp.arange(degree_total, dtype=j...]
    all_to_all x1, waiting for transfers between devices: 137 us -> 69.9 us  [per_device(): lax.all_to_all(increment, 'lev', split_axis=2, concat_axis=1, tiled=True)]
    while x224 -> x0, other arithmetic: 45.5 us -> none
    dot_general x3 -> x2, matrix products: 53.4 us -> 9.13 us  [the longest x1 4.86 us: per_device(): jnp.einsum('mclj,cmx->jlx', fourier, dft_table, preferred_element_type=jn...]
    pallas_call x0 -> x2, Pallas kernels: none -> 34.7 us  [the longest x1 28.1 us: synthesis(): pl.pallas_call(functools.partial(synthesis_kernel, half_lats), grid=(wave...]
    dynamic_update_slice x32 -> x0, local copies, waits for them, and re-layouts: 31 us -> none  [legendre_table(): lax.scan(advance, (zeros, zeros, zeros), jnp.arange(degree_total, dtype=j...]
    all_to_all x6 -> x0, local copies, waits for them, and re-layouts: 29.5 us -> none  [the longest x2 14.7 us: per_device(): lax.all_to_all(increment, 'lev', split_axis=2, concat_axis=1, tiled=True)]
    unnamed x1 -> x0, matrix products: 26.8 us -> none
  transfers between devices with their start and end apart: 2 -> 2, of which waited for: 2 -> 2; matrix products, arithmetic and copies ran while one was open for 0% -> 1% of each run, Pallas kernels for 0% -> 0%
where the time goes in v1:
time: 378 us; the launch traced here: 377 us
  blocking collectives  104 us (28%)
  waiting for transfers between devices  92.8 us (25%)
  local copies, waits for them, and re-layouts  57 us (15%)
  matrix products  45.5 us (12%)
  Pallas kernels  34.7 us (9%)
  other arithmetic  30.2 us (8%)
  starting transfers between devices  11.3 us (3%)
    all_to_all x1, blocking collectives, per_device(): lax.all_to_all(jnp.transpose(grid_grad, (0, 2, 1)).astype(jnp.bfloat16),...  74.5 us
    all_to_all x1, waiting for transfers between devices, per_device(): lax.all_to_all(increment, 'lev', split_axis=2, concat_axis=1, tiled=True)  69.9 us
    all_to_all x1, blocking collectives, per_device(): lax.all_to_all(coeff_grad, 'lat', split_axis=0, concat_axis=0, tiled=True)  29.3 us
    pallas_call x1, Pallas kernels, synthesis(): pl.pallas_call(functools.partial(synthesis_kernel, half_lats), grid=(wave...  28.1 us
    all_to_all x1, waiting for transfers between devices, per_device(): lax.all_to_all(fourier, 'lat', split_axis=0, concat_axis=0, tiled=True)  22.9 us
    dot_general x1, matrix products, radiance_pass(): jnp.dot(misfit, weight_out.T, preferred_element_type=jnp.float32)  15.1 us
    scatter-add x1, other arithmetic, per_device(): jnp.zeros(cell_rows.shape, jnp.float32).at[local_cols]  14.3 us
    convert_element_type x2, local copies, waits for them, and re-layouts, per_device(): increment = jnp.transpose(increment, (0, 2, 1)).astype(jnp.float32)  14.2 us
  transfers between devices with their start and end apart: 2, of which 2 were waited for; matrix products, arithmetic and copies ran while one was open for 1% of the time, Pallas kernels for 0%

profile of v1, /device:TPU:0, one launch (start us, length us, event | category | flops | bytes accessed | tf_op | source)
XLA Modules:
  0.0 376.7 jit_solution(1275935543085838641)
XLA Ops:
  1.5 1.7 convert_bitcast_fusion.1
  3.8 0.8 sqrt_multiply_fusion
  4.7 28.1 %shard_map.113 = (bf16[64,256,256]{2,1,0:T(8,128)(2,1)S(1)}, bf16[4,64,32,96]{3,2,1,0:T(8,128)(2,1)S(1)}) custom-call(f32[32,64,8]{2,1,0:T(8,128)S(1)} %get-tuple-element.9.fa_ref, f32[32,64,8]{2,1,0:T(8,128)S(1)} %get-tuple-element.8.fb_ref, f32[64,256]{1,0:T(8,128)S(1)} %pad.11.log_ref, f32[1,256]{1,0:T(1,128)S(1)} %bitcast.72, f32[1,256]{1,0:T(1,128)S(1)} %bitcast.71, ...), custom_call_target="tpu_custom_call" | custom-call | tf_op jit(solution)/shard_map/pallas_call | solution.py:161
  32.9 3.2 copy-done.1
  36.1 1.3 copy-done.3
  37.4 4.5 %all-to-all-start = ((bf16[4,64,32,96]{3,2,1,0:T(8,128)(2,1)}), bf16[4,64,32,96]{3,2,1,0:T(8,128)(2,1)}, u32[]{:S(2)}, u32[]{:S(2)}) async-start(bf16[4,64,32,96]{3,2,1,0:T(8,128)(2,1)} %copy-done.3), calls=%async_computation | async-start | bytes 4194304 | tf_op jit(solution)/shard_map/all_to_all | solution.py:258
  41.9 3.4 multiply_convert_fusion.10
  45.3 22.9 %all-to-all-done = bf16[4,64,32,96]{3,2,1,0:T(8,128)(2,1)} async-done(((bf16[4,64,32,96]{3,2,1,0:T(8,128)(2,1)}), bf16[4,64,32,96]{3,2,1,0:T(8,128)(2,1)}, u32[]{:S(2)}, u32[]{:S(2)}) %all-to-all-start) | async-done | bytes 1572896 | tf_op jit(solution)/shard_map/all_to_all | solution.py:258
  68.2 4.9 %fusion.8 = bf16[96,16,768]{2,0,1:T(8,128)(2,1)} fusion(bf16[256,2,16,96]{3,2,1,0:T(8,128)(2,1)} %bitcast.4, bf16[1,256,768]{2,1,0:T(8,128)(2,1)S(1)} %get-tuple-element.14, bf16[1,256,768]{2,1,0:T(8,128)(2,1)S(1)} %get-tuple-element.15), kind=kOutput, calls=%fused_computation.21 | convolution fusion | flops 1210712064 | bytes 4718592 | tf_op jit(solution)/shard_map/mclj,cmx->jlx/dot_general | solution.py:262
  73.1 4.8 %copy.66 = bf16[96,16,768]{0,1,2:T(8,128)(2,1)} copy(bf16[96,16,768]{2,0,1:T(8,128)(2,1)} %fusion.8) | data formatting | bytes 4718592 | tf_op jit(solution)/shard_map/convert_element_type | solution.py:264
  77.9 6.8 %all-to-all-start.1 = ((bf16[96,16,768]{0,1,2:T(8,128)(2,1)}), bf16[96,16,768]{0,1,2:T(8,128)(2,1)}, u32[]{:S(2)}, u32[]{:S(2)}) async-start(bf16[96,16,768]{0,1,2:T(8,128)(2,1)} %copy.66), calls=%async_computation.1 | async-start | bytes 6291456 | tf_op jit(solution)/shard_map/all_to_all | solution.py:265
  85.5 69.9 %all-to-all-done.1 = bf16[96,16,768]{0,1,2:T(8,128)(2,1)} async-done(((bf16[96,16,768]{0,1,2:T(8,128)(2,1)}), bf16[96,16,768]{0,1,2:T(8,128)(2,1)}, u32[]{:S(2)}, u32[]{:S(2)}) %all-to-all-start.1) | async-done | bytes 2359328 | tf_op jit(solution)/shard_map/all_to_all | solution.py:265
  155.3 8.1 %copy.67 = f32[96,16,8,96]{3,1,2,0:T(8,128)} copy(bf16[96,16,8,96]{0,1,3,2:T(8,128)(2,1)} %bitcast.32) | data formatting | bytes 7077888 | tf_op jit(solution)/shard_map/convert_element_type | solution.py:266
  163.4 6.1 %copy.68 = f32[96,128,96]{1,2,0:T(8,128)} copy(f32[96,128,96]{2,1,0:T(8,128)} %bitcast.73) | data formatting | bytes 9437184 | tf_op jit(solution)/shard_map/convert_element_type | solution.py:266
  169.6 5.3 %fusion = bf16[96,96,128]{2,1,0:T(8,128)(2,1)} fusion(f32[96,128,96]{1,2,0:T(8,128)} %copy.68, bf16[96,96,128]{2,1,0:T(8,128)(2,1)} %param.11), kind=kLoop, calls=%fused_computation.9 | loop fusion | flops 3538944 | bytes 9437184 | tf_op jit(solution)/shard_map/convert_element_type | solution.py:267
  174.8 7.6 %gather_fusion = bf16[2048,128]{1,0:T(8,128)(2,1)S(1)} fusion(bf16[9216,128]{1,0:T(8,128)(2,1)} %bitcast.76, s32[2048]{0:T(1024)S(1)} %broadcast_clamp_fusion), kind=kCustom, calls=%fused_computation | custom fusion | bytes 1056768 | tf_op jit(solution)/shard_map/jit(_take)/gather | solution.py:272
  182.4 2.3 fusion.26
  184.7 6.7 %fusion.4 = f32[2048,1024]{1,0:T(8,128)} fusion(bf16[1024,1024]{1,0:T(8,128)(2,1)S(1)} %copy-done, f32[2048,1024]{1,0:T(8,128)S(1)} %fusion.26), kind=kOutput, calls=%fused_computation.16 | convolution fusion | flops 4305453056 | bytes 18874368 | tf_op jit(solution)/shard_map/dot_general | solution.py:223
  191.4 15.1 %multiply_convert_fusion.1 = bf16[2048,1024]{1,0:T(8,128)(2,1)} fusion(f32[2048,1024]{1,0:T(8,128)} %fusion.4, bf16[1024,512]{1,0:T(8,128)(2,1)} %param.19, bf16[1,2048,512]{2,1,0:T(8,128)(2,1)} %param.14, f32[512]{0:T(512)S(1)} %copy-done.8, f32[2048]{0:T(1024)S(1)} %bitcast.83, pred[2048]{0:T(1024)(128)(4,1)S(1)} %iota_compare_fusion.1), kind=kOutput, calls=%fused_computation.3 | convolution fusion | flops 4331667456 | bytes 15740928 | tf_op jit(solution)/shard_map/dot_general | solution.py:232
  206.5 12.3 %fusion.7 = f32[2048,128]{1,0:T(8,128)} fusion(bf16[128,1024]{1,0:T(8,128)(2,1)S(1)} %copy-done.5, f32[2048,1024]{1,0:T(8,128)} %copy-done.4, bf16[2048,1024]{1,0:T(8,128)(2,1)} %multiply_convert_fusion.1, bf16[1024,1024]{1,0:T(8,128)(2,1)S(1)} %copy-done), kind=kOutput, calls=%fused_computation.20 | convolution fusion | flops 4851236864 | bytes 15990784 | tf_op jit(solution)/shard_map/dot_general | solution.py:238
  218.8 14.3 %scatter_custom_fusion = f32[9216,128]{1,0:T(8,128)} fusion(s32[2048]{0:T(1024)S(1)} %bitcast.82, f32[2048,128]{1,0:T(8,128)} %fusion.7, f32[]{:T(128)} %constant.37.clone.1), kind=kCustom, calls=%fused_computation.23 | custom fusion | flops 262144 | bytes 4719104 | tf_op jit(solution)/shard_map/scatter-add | solution.py:281
  233.0 4.3 %convert_bitcast_fusion = bf16[96,128,96]{1,2,0:T(8,128)(2,1)} fusion(f32[96,96,128]{2,1,0:T(8,128)} %bitcast.74), kind=kLoop, calls=%fused_computation.22 | loop fusion | flops 1179648 | bytes 7077888 | tf_op jit(solution)/shard_map/convert_element_type | solution.py:285
  237.3 4.8 %copy.69 = bf16[96,128,96]{2,0,1:T(8,128)(2,1)} copy(bf16[96,128,96]{1,2,0:T(8,128)(2,1)} %convert_bitcast_fusion) | data formatting | bytes 4718592 | tf_op jit(solution)/shard_map/convert_element_type | solution.py:285
  242.1 74.5 %all_to_all.37 = bf16[96,128,96]{2,0,1:T(8,128)(2,1)S(1)} all-to-all(bf16[96,128,96]{2,0,1:T(8,128)(2,1)} %copy.69), channel_id=1, replica_groups=mesh['lat'=4,'lev'=8] {'lev'}, dimensions={1} | all-to-all | bytes 4718592 | tf_op jit(solution)/shard_map/all_to_all | solution.py:284
  316.6 3.7 copy.71
  320.4 6.0 %reshape.329 = bf16[96,16,768,1]{2,0,1,3:T(8,128)(2,1)} reshape(bf16[96,16,8,96]{3,2,0,1:T(8,128)(2,1)} %copy.71) | data formatting | bytes 4718592 | tf_op jit(solution)/shard_map/all_to_all | solution.py:284
  326.3 4.3 %fusion.18 = bf16[256,2,16,96]{0,3,2,1:T(8,128)(2,1)} fusion(bf16[96,16,768,1]{2,0,1,3:T(8,128)(2,1)} %reshape.329, bf16[1,256,768]{2,1,0:T(8,128)(2,1)S(1)} %get-tuple-element.14, bf16[1,256,768]{2,1,0:T(8,128)(2,1)S(1)} %get-tuple-element.15), kind=kOutput, calls=%fused_computation.33 | convolution fusion | flops 1210318848 | bytes 4718592 | tf_op jit(solution)/shard_map/jlx,cmx->mclj/dot_general | solution.py:291
  330.6 4.4 %copy.72 = bf16[256,2,16,96]{3,2,1,0:T(8,128)(2,1)} copy(bf16[256,2,16,96]{0,3,2,1:T(8,128)(2,1)} %fusion.18) | data formatting | bytes 3145728 | tf_op jit(solution)/shard_map/convert_element_type | solution.py:293
  335.0 29.3 %all_to_all.38.coeff_ref = bf16[4,64,32,96]{3,2,1,0:T(8,128)(2,1)S(1)} all-to-all(bf16[4,64,32,96]{3,2,1,0:T(8,128)(2,1)} %bitcast.78), channel_id=1, replica_groups=mesh['lat'=4,'lev'=8] {'lat'}, dimensions={0} | all-to-all | bytes 3145728 | tf_op jit(solution)/shard_map/all_to_all | solution.py:295
  364.3 3.4 copy-done.2
  367.7 6.5 %shard_map.114 = f32[64,32,256]{2,1,0:T(8,128)S(1)} custom-call(bf16[4,64,32,96]{3,2,1,0:T(8,128)(2,1)S(1)} %all_to_all.38.coeff_ref, bf16[64,256,256]{2,1,0:T(8,128)(2,1)S(1)} %copy-done.2), custom_call_target="tpu_custom_call" | custom-call | tf_op jit(solution)/shard_map/pallas_call | solution.py:190
  374.2 2.5 copy.80
  (44 shorter events, 1.5 us)
Async XLA Ops:
  0.6 184.0 %copy-start = (bf16[1024,1024]{1,0:T(8,128)(2,1)S(1)}, bf16[1024,1024]{1,0:T(8,128)(2,1)}, u32[]{:S(2)}) copy-start(bf16[1024,1024]{1,0:T(8,128)(2,1)} %param.18) | copy-start | bytes 6291460
  32.9 3.2 copy-start.1
  36.1 1.3 copy-start.3
  37.4 30.8 %all-to-all-start = ((bf16[4,64,32,96]{3,2,1,0:T(8,128)(2,1)}), bf16[4,64,32,96]{3,2,1,0:T(8,128)(2,1)}, u32[]{:S(2)}, u32[]{:S(2)}) async-start(bf16[4,64,32,96]{3,2,1,0:T(8,128)(2,1)} %copy-done.3), calls=%async_computation | async-start | bytes 4194304 | tf_op jit(solution)/shard_map/all_to_all | solution.py:258
  77.9 7.5 %copy-start.6 = (s32[1,2048]{1,0:T(1,128)S(1)}, s32[1,2048]{1,0:T(1,128)}, u32[]{:S(2)}) copy-start(s32[1,2048]{1,0:T(1,128)} %param.12) | copy-start | bytes 24580
  77.9 7.5 %copy-start.7 = (s32[1,2048]{1,0:T(1,128)S(1)}, s32[1,2048]{1,0:T(1,128)}, u32[]{:S(2)}) copy-start(s32[1,2048]{1,0:T(1,128)} %param.15) | copy-start | bytes 24580
  77.9 77.4 %all-to-all-start.1 = ((bf16[96,16,768]{0,1,2:T(8,128)(2,1)}), bf16[96,16,768]{0,1,2:T(8,128)(2,1)}, u32[]{:S(2)}, u32[]{:S(2)}) async-start(bf16[96,16,768]{0,1,2:T(8,128)(2,1)} %copy.66), calls=%async_computation.1 | async-start | bytes 6291456 | tf_op jit(solution)/shard_map/all_to_all | solution.py:265
  184.7 6.7 %copy-start.4 = (f32[2048,1024]{1,0:T(8,128)}, f32[2048,1024]{1,0:T(8,128)S(1)}, u32[]{:S(2)}) copy-start(f32[2048,1024]{1,0:T(8,128)S(1)} %fusion.26) | copy-start | bytes 25165828
  184.7 6.7 %copy-start.8 = (f32[512]{0:T(512)S(1)}, f32[512]{0:T(512)}, u32[]{:S(2)}) copy-start(f32[512]{0:T(512)} %param.16) | copy-start | bytes 6148
  191.4 15.1 %copy-start.5 = (bf16[128,1024]{1,0:T(8,128)(2,1)S(1)}, bf16[128,1024]{1,0:T(8,128)(2,1)}, u32[]{:S(2)}) copy-start(bf16[128,1024]{1,0:T(8,128)(2,1)} %param.17) | copy-start | bytes 786436
  364.3 3.4 copy-start.2

commit v2 on v1

--- a/solution.py
+++ b/solution.py
@@ -200,6 +200,87 @@
     )(coeffs, table)
 
 
+def pick_kernel(index_ref, shift_ref, count_ref, grid_ref, out_ref):
+    target = pl.program_id(0)
+    levels, capacity = out_ref.shape[1:]
+    out_ref[...] = jnp.zeros(out_ref.shape, out_ref.dtype)
+    lane = lax.broadcasted_iota(jnp.int32, (levels, HALF), 1)
+
+    def block(b, carry):
+        base = b * HALF
+        total = jnp.zeros((levels, HALF), jnp.float32)
+        for q in range(HALF):
+            at = target * capacity + base + q
+            moved = pltpu.roll(grid_ref[index_ref[at]], shift_ref[at], 1)
+            total = jnp.where(lane == q, moved, total)
+        out_ref[0, :, pl.ds(pl.multiple_of(base, HALF), HALF)] = total.astype(out_ref.dtype)
+        return carry
+
+    lax.fori_loop(0, (count_ref[target] + HALF - 1) // HALF, block, 0)
+
+
+def pick(index, shift, counts, grid, capacity):
+    owners = counts.shape[0]
+    levels = grid.shape[1]
+    return pl.pallas_call(
+        pick_kernel,
+        grid_spec=pltpu.PrefetchScalarGridSpec(
+            num_scalar_prefetch=3,
+            grid=(owners,),
+            in_specs=[pl.BlockSpec(grid.shape, lambda t, *_: (0, 0, 0))],
+            out_specs=pl.BlockSpec((1, levels, capacity), lambda t, *_: (t, 0, 0)),
+        ),
+        out_shape=jax.ShapeDtypeStruct((owners, levels, capacity), jnp.bfloat16),
+        compiler_params=pltpu.CompilerParams(vmem_limit_bytes=32 << 20),
+    )(index, shift, counts, grid)
+
+
+def spread_kernel(row_ref, lane_ref, count_ref, values_ref, out_ref, *sums):
+    owners, levels, capacity = values_ref.shape
+    lane = lax.broadcasted_iota(jnp.int32, (levels, HALF), 1)
+    most = count_ref[0]
+    for o in range(owners):
+        sums[o][...] = jnp.zeros(sums[o].shape, jnp.float32)
+        most = jnp.maximum(most, count_ref[o])
+
+    def one(slot, carry):
+        base = pl.multiple_of((slot // HALF) * HALF, HALF)
+        spot = slot % HALF
+        for o in range(owners):
+            row = row_ref[o * capacity + slot]
+            to = lane_ref[o * capacity + slot]
+            values = values_ref[o, :, pl.ds(base, HALF)]
+            moved = pltpu.roll(values, (to - spot + HALF) % HALF, 1)
+            sums[o][row] = sums[o][row] + jnp.where(lane == to, moved, 0.0)
+        return carry
+
+    def several(group, carry):
+        for k in range(4):
+            one(group * 4 + k, carry)
+        return carry
+
+    lax.fori_loop(0, (most + 3) // 4, several, 0)
+    for o in range(owners):
+        out_ref[o] = sums[o][...].astype(out_ref.dtype)
+
+
+def spread(rows, lanes, counts, values, band_rows):
+    owners, levels, capacity = values.shape
+    shape = (owners, band_rows, levels, HALF)
+    return pl.pallas_call(
+        spread_kernel,
+        grid_spec=pltpu.PrefetchScalarGridSpec(
+            num_scalar_prefetch=3,
+            grid=(1,),
+            in_specs=[pl.BlockSpec(values.shape, lambda g, *_: (0, 0, 0))],
+            out_specs=pl.BlockSpec(shape, lambda g, *_: (0, 0, 0, 0)),
+            scratch_shapes=[pltpu.VMEM(shape[1:], jnp.float32) for _ in range(owners)],
+        ),
+        out_shape=jax.ShapeDtypeStruct(shape, jnp.bfloat16),
+        compiler_params=pltpu.CompilerParams(vmem_limit_bytes=40 << 20),
+    )(rows, lanes, counts, values)
+
+
 def wave_table(wave_total, lon_total):
     wave_ids = jnp.arange(wave_total, dtype=jnp.int32)
     lon_ids = jnp.arange(lon_total, dtype=jnp.int32)
@@ -259,18 +340,31 @@
     band = fourier.shape[3]
     fourier = fourier.reshape(M, parts, levels, band)
     dft_table = wave_table(M, NLON).astype(jnp.bfloat16)
+    band_rows, tile_cols, all_levels = background.shape
+    local_cols = columns[0]
+    owners = all_levels // levels
+    capacity = local_cols.shape[0]
+    listed = lax.all_gather(local_cols, "lev")
+    band_counts = lax.all_gather(counts, "lev", tiled=True)
+    tiles = NLON // HALF
+    list_rows = listed // tile_cols
+    list_lanes = listed % tile_cols
+    list_lons = list_lanes + jnp.arange(owners, dtype=jnp.int32)[:, None] * tile_cols
+    spots = jnp.arange(capacity, dtype=jnp.int32) % HALF
+    index = (list_rows * tiles + list_lons // HALF).reshape(-1)
+    shift = ((spots[None, :] - list_lons) % HALF).reshape(-1)
     increment = jnp.einsum(
-        "mclj,cmx->jlx", fourier, dft_table, preferred_element_type=jnp.float32
-    ).astype(jnp.bfloat16)
-    increment = lax.all_to_all(increment, "lev", split_axis=2, concat_axis=1, tiled=True)
-    increment = jnp.transpose(increment, (0, 2, 1)).astype(jnp.float32)
-    grid_state = (background.astype(jnp.float32) + increment).astype(jnp.bfloat16)
-    band_rows = grid_state.shape[0]
-    tile_cols = grid_state.shape[1]
-    cell_rows = grid_state.reshape(band_rows * tile_cols, grid_state.shape[2])
-    local_cols = columns[0]
-    profiles = jnp.take(cell_rows, local_cols, axis=0)
-    capacity = local_cols.shape[0]
+        "mclj,cmtx->jtlx",
+        fourier,
+        dft_table.reshape(parts, M, tiles, HALF),
+        preferred_element_type=jnp.float32,
+    ).reshape(band * tiles, levels, HALF)
+    picked = pick(index, shift, band_counts, increment, capacity)
+    picked = lax.all_to_all(picked, "lev", split_axis=0, concat_axis=0, tiled=True)
+    picked = picked.reshape(all_levels, capacity)
+    cell_rows = background.reshape(band_rows * tile_cols, all_levels)
+    own_rows = jnp.take(cell_rows, local_cols, axis=0).astype(jnp.float32)
+    profiles = (own_rows + picked.T.astype(jnp.float32)).astype(jnp.bfloat16)
     usable = jnp.arange(capacity, dtype=jnp.int32) < counts[0]
     observed = radiances[0]
     pair_counts = used_pairs[0].astype(jnp.float32)
@@ -280,16 +374,20 @@
     grid_grad = (
         jnp.zeros(cell_rows.shape, jnp.float32).at[local_cols].add(block_grad.astype(jnp.float32))
     )
-    grid_grad = grid_grad.reshape(band_rows, tile_cols, cell_rows.shape[1])
-    grad_rows = lax.all_to_all(
-        jnp.transpose(grid_grad, (0, 2, 1)).astype(jnp.bfloat16),
-        "lev",
-        split_axis=1,
-        concat_axis=2,
-        tiled=True,
-    )
+    grid_grad = grid_grad.reshape(band_rows, tile_cols, all_levels)
+    sent = block_grad.T.reshape(owners, levels, capacity)
+    sent = lax.all_to_all(sent, "lev", split_axis=0, concat_axis=0, tiled=True)
+    grad_rows = spread(
+        list_rows.reshape(-1),
+        list_lanes.reshape(-1),
+        band_counts,
+        sent.astype(jnp.float32),
+        band_rows,
+    )
+    tile_table = dft_table.reshape(parts, M, owners, tile_cols)
+    tile_table = jnp.pad(tile_table, ((0, 0), (0, 0), (0, 0), (0, HALF - tile_cols)))
     coeff_grad = jnp.einsum(
-        "jlx,cmx->mclj", grad_rows, dft_table, preferred_element_type=jnp.float32
+        "ojlx,cmox->mclj", grad_rows, tile_table, preferred_element_type=jnp.float32
     ).astype(jnp.bfloat16)
     coeff_grad = coeff_grad.reshape(bands, waves_local, parts * levels, band)
     coeff_grad = lax.all_to_all(coeff_grad, "lat", split_axis=0, concat_axis=0, tiled=True)

time: 378 us -> 351 us (0.929)
  Pallas kernels: 34.7 us -> 169 us
  waiting for transfers between devices: 92.8 us -> 17.6 us
  blocking collectives: 104 us -> 43.1 us
  local copies, waits for them, and re-layouts: 57 us -> 34.5 us
  matrix products: 45.5 us -> 40.3 us
  starting transfers between devices: 11.3 us -> 16.3 us
    pallas_call x0 -> x2, Pallas kernels: none -> 134 us  [the longest x1 111 us: spread(): pl.pallas_call(spread_kernel, grid_spec=pltpu.PrefetchScalarGridSpec(num_...]
    all_to_all x2 -> x0, blocking collectives: 104 us -> none  [the longest x1 74.5 us: per_device(): lax.all_to_all(jnp.transpose(grid_grad, (0, 2, 1)).astype(jnp.bfloat16),...]
    all_to_all x1 -> x3, waiting for transfers between devices: 69.9 us -> 17.6 us  [the longest x1 10.2 us: per_device(): lax.all_to_all(coeff_grad, 'lat', split_axis=0, concat_axis=0, tiled=True)]
    all_gather x0 -> x1, blocking collectives: none -> 32.3 us  [per_device(): listed = lax.all_gather(local_cols, 'lev')]
    convert_element_type x5 -> x3, local copies, waits for them, and re-layouts: 28.3 us -> 4.57 us  [the longest x1 3 us: per_device(): coeff_grad = jnp.einsum('ojlx,cmox->mclj', grad_rows, tile_table, preferr...]
    all_to_all x1, waiting for transfers between devices: 22.9 us -> 0.01 us  [per_device(): lax.all_to_all(fourier, 'lat', split_axis=0, concat_axis=0, tiled=True)]
    unnamed x0 -> x1, blocking collectives: none -> 10.8 us
    all_to_all x2 -> x0, local copies, waits for them, and re-layouts: 9.71 us -> none  [per_device(): lax.all_to_all(jnp.transpose(grid_grad, (0, 2, 1)).astype(jnp.bfloat16),...]
  transfers between devices with their start and end apart: 2 -> 4, of which waited for: 2 -> 3; matrix products, arithmetic and copies ran while one was open for 1% -> 10% of each run, Pallas kernels for 0% -> 0%
where the time goes in v2:
time: 351 us; the launch traced here: 349 us
  Pallas kernels  169 us (48%)
  blocking collectives  43.1 us (12%)
  matrix products  40.3 us (11%)
  local copies, waits for them, and re-layouts  34.5 us (10%)
  other arithmetic  27.4 us (8%)
  waiting for transfers between devices  17.6 us (5%)
  starting transfers between devices  16.3 us (5%)
    pallas_call x1, Pallas kernels, spread(): pl.pallas_call(spread_kernel, grid_spec=pltpu.PrefetchScalarGridSpec(num_...  111 us
    all_gather x1, blocking collectives, per_device(): listed = lax.all_gather(local_cols, 'lev')  32.3 us
    pallas_call x1, Pallas kernels, synthesis(): pl.pallas_call(functools.partial(synthesis_kernel, half_lats), grid=(wave...  28.1 us
    pallas_call x1, Pallas kernels, pick(): pl.pallas_call(pick_kernel, grid_spec=pltpu.PrefetchScalarGridSpec(num_sc...  23 us
    scatter-add x1, other arithmetic, per_device(): jnp.zeros(cell_rows.shape, jnp.float32).at[local_cols]  14 us
    dot_general x1, matrix products, radiance_pass(): jnp.dot(misfit, weight_out.T, preferred_element_type=jnp.float32)  13.7 us
    dot_general x1, matrix products, radiance_pass(): jnp.dot(back_first, weight_in.T, preferred_element_type=jnp.float32)  12.8 us
    unnamed x41, local copies, waits for them, and re-layouts  12.3 us
  transfers between devices with their start and end apart: 4, of which 3 were waited for; matrix products, arithmetic and copies ran while one was open for 10% of the time, Pallas kernels for 0%

profile of v2, /device:TPU:0, one launch (start us, length us, event | category | flops | bytes accessed | tf_op | source)
XLA Modules:
  0.0 349.5 jit_solution(10299368475257256792)
XLA Ops:
  1.5 1.7 convert_bitcast_fusion
  4.8 28.1 %shard_map.113 = (bf16[64,256,256]{2,1,0:T(8,128)(2,1)S(1)}, bf16[4,64,32,96]{3,2,1,0:T(8,128)(2,1)S(1)}) custom-call(f32[32,64,8]{2,1,0:T(8,128)S(1)} %get-tuple-element.11.fa_ref, f32[32,64,8]{2,1,0:T(8,128)S(1)} %get-tuple-element.10.fb_ref, f32[64,256]{1,0:T(8,128)S(1)} %pad.16.log_ref, f32[1,256]{1,0:T(1,128)S(1)} %bitcast.137, f32[1,256]{1,0:T(1,128)S(1)} %bitcast.138, ...), custom_call_target="tpu_custom_call" | custom-call | tf_op jit(solution)/shard_map/pallas_call | solution.py:161
  32.9 3.2 copy-done.2
  37.5 4.5 %all-to-all-start = ((bf16[4,64,32,96]{3,2,1,0:T(8,128)(2,1)}), bf16[4,64,32,96]{3,2,1,0:T(8,128)(2,1)}, u32[]{:S(2)}, u32[]{:S(2)}) async-start(bf16[4,64,32,96]{3,2,1,0:T(8,128)(2,1)} %copy-done.6), calls=%async_computation | async-start | bytes 4194304 | tf_op jit(solution)/shard_map/all_to_all | solution.py:339
  42.0 32.3 %all-gather = s32[8,1,2048]{2,1,0:T(1,128)S(1)} all-gather(s32[1,1,2048]{2,1,0:T(1,128)S(1)} %bitcast.142), channel_id=1, replica_groups=mesh['lat'=4,'lev'=8] {'lev'}, dimensions={0}, use_global_device_ids=true | all-gather | bytes 73728 | tf_op jit(solution)/shard_map/all_gather | solution.py:347
  76.5 10.8 %all-reduce.4.count_ref = s32[8]{0:T(128)S(1)} all-reduce(s32[8]{0:T(128)S(1)} %dynamic-update-slice), channel_id=1, replica_groups=mesh['lat'=4,'lev'=8] {'lev'}, use_global_device_ids=true, to_apply=%add.4 | all-reduce | flops 8 | bytes 64
  87.5 3.4 multiply_convert_fusion.13
  91.5 4.2 %copy.65 = bf16[256,2,16,96]{0,3,1,2:T(8,128)(2,1)} copy(bf16[256,2,16,96]{3,2,1,0:T(8,128)(2,1)} %bitcast.18) | data formatting | bytes 3145728 | tf_op jit(solution)/shard_map/reshape | solution.py:341
  95.7 2.8 convolution_bitcast_fusion
  98.5 2.7 copy.66
  101.3 23.0 %shard_map.114 = bf16[8,16,2048]{2,1,0:T(8,128)(2,1)} custom-call(s32[16384]{0:T(1024)S(1)} %bitcast.133, s32[16384]{0:T(1024)S(1)} %bitcast.134, s32[8]{0:T(128)S(1)} %all-reduce.4.count_ref, f32[576,16,128]{2,1,0:T(8,128)S(1)} %bitcast.130), custom_call_target="tpu_custom_call" | custom-call | tf_op jit(solution)/shard_map/pallas_call | solution.py:225
  124.3 3.7 %all-to-all-start.1 = ((bf16[8,16,2048]{2,1,0:T(8,128)(2,1)}), bf16[8,16,2048]{2,1,0:T(8,128)(2,1)S(1)}, u32[]{:S(2)}, u32[]{:S(2)}) async-start(bf16[8,16,2048]{2,1,0:T(8,128)(2,1)} %shard_map.114), calls=%async_computation.1 | async-start | bytes 1048576 | tf_op jit(solution)/shard_map/all_to_all | solution.py:363
  128.6 7.2 %gather_fusion = bf16[2048,128]{1,0:T(8,128)(2,1)S(1)} fusion(bf16[9216,128]{1,0:T(8,128)(2,1)S(1)} %bitcast.129, s32[2048]{0:T(1024)} %broadcast_clamp_fusion), kind=kCustom, calls=%fused_computation | custom fusion | bytes 1056768 | tf_op jit(solution)/shard_map/jit(_take)/gather | solution.py:366
  136.5 1.7 all-to-all-done.1
  138.6 2.4 fusion.45
  141.1 6.8 %fusion.3 = f32[2048,1024]{1,0:T(8,128)} fusion(bf16[1024,1024]{1,0:T(8,128)(2,1)S(1)} %copy-done.13, f32[2048,1024]{1,0:T(8,128)S(1)} %fusion.45), kind=kOutput, calls=%fused_computation.13 | convolution fusion | flops 4305453056 | bytes 18874368 | tf_op jit(solution)/shard_map/dot_general | solution.py:304
  147.9 13.7 %multiply_convert_fusion.1 = bf16[2048,1024]{1,0:T(8,128)(2,1)} fusion(f32[2048,1024]{1,0:T(8,128)} %fusion.3, bf16[1024,512]{1,0:T(8,128)(2,1)S(1)} %copy-done.14, bf16[1,2048,512]{2,1,0:T(8,128)(2,1)} %param.14, f32[512]{0:T(512)S(1)} %copy-done.15, f32[2048]{0:T(1024)S(1)} %bitcast.146, pred[2048]{0:T(1024)(128)(4,1)S(1)} %iota_compare_fusion.2), kind=kOutput, calls=%fused_computation.3 | convolution fusion | flops 4331667456 | bytes 15740928 | tf_op jit(solution)/shard_map/dot_general | solution.py:313
  161.6 12.8 %convolution_convert_fusion = bf16[2048,128]{0,1:T(8,128)(2,1)} fusion(bf16[128,1024]{1,0:T(8,128)(2,1)S(1)} %copy-done.8, f32[2048,1024]{1,0:T(8,128)} %copy-done.7, bf16[2048,1024]{1,0:T(8,128)(2,1)} %multiply_convert_fusion.1, bf16[1024,1024]{1,0:T(8,128)(2,1)} %param.18), kind=kOutput, calls=%fused_computation.20 | convolution fusion | flops 4850974720 | bytes 15466496 | tf_op jit(solution)/shard_map/dot_general | solution.py:319
  174.4 4.3 %all-to-all-start.2 = ((bf16[8,16,2048]{2,1,0:T(8,128)(2,1)}), bf16[8,16,2048]{2,1,0:T(8,128)(2,1)S(1)}, u32[]{:S(2)}, u32[]{:S(2)}) async-start(bf16[8,16,2048]{2,1,0:T(8,128)(2,1)} %bitcast.28), calls=%async_computation.2 | async-start | bytes 1048576 | tf_op jit(solution)/shard_map/all_to_all | solution.py:379
  178.7 4.5 %multiply_convert_fusion.11 = (bf16[1,256,8,96]{3,1,2,0:T(8,128)(2,1)S(1)}, bf16[1,256,8,96]{3,1,2,0:T(8,128)(2,1)S(1)}) fusion(s32[8,96]{1,0:T(8,128)S(1)} %multiply_add_fusion.3, f32[256]{0:T(256)S(1)} %get-tuple-element.20, f32[256]{0:T(256)S(1)} %copy-done.12), kind=kLoop, calls=%fused_computation.50 | loop fusion | flops 2555904 | bytes 791552 | tf_op jit(solution)/shard_map/convert.5
  183.2 5.7 %all-to-all-done.2 = bf16[8,16,2048]{2,1,0:T(8,128)(2,1)S(1)} async-done(((bf16[8,16,2048]{2,1,0:T(8,128)(2,1)}), bf16[8,16,2048]{2,1,0:T(8,128)(2,1)S(1)}, u32[]{:S(2)}, u32[]{:S(2)}) %all-to-all-start.2) | async-done | bytes 524320 | tf_op jit(solution)/shard_map/all_to_all | solution.py:379
  189.0 110.9 %shard_map.115 = bf16[8,96,16,128]{3,2,1,0:T(8,128)(2,1)S(1)} custom-call(s32[16384]{0:T(1024)S(1)} %bitcast.135, s32[16384]{0:T(1024)S(1)} %bitcast.136, s32[8]{0:T(128)S(1)} %all-reduce.4.count_ref, f32[8,16,2048]{2,1,0:T(8,128)S(1)} %convert_element_type.135.values_ref), custom_call_target="tpu_custom_call" | custom-call | tf_op jit(solution)/shard_map/pallas_call | solution.py:270
  299.9 1.9 fusion.22
  301.8 3.0 copy.69
  304.8 3.8 %all-to-all-start.3 = ((bf16[4,64,32,96]{3,2,1,0:T(8,128)(2,1)}), bf16[4,64,32,96]{3,2,1,0:T(8,128)(2,1)S(1)}, u32[]{:S(2)}, u32[]{:S(2)}) async-start(bf16[4,64,32,96]{3,2,1,0:T(8,128)(2,1)} %bitcast.139), calls=%async_computation.3 | async-start | bytes 4194304 | tf_op jit(solution)/shard_map/all_to_all | solution.py:393
  309.9 14.0 %scatter_custom_fusion = f32[9216,128]{1,0:T(8,128)} fusion(s32[2048]{0:T(1024)} %bitcast.144, f32[2048,128]{1,0:T(8,128)S(1)} %copy.71, f32[]{:T(128)} %constant.137.clone.1), kind=kCustom, calls=%fused_computation.21 | custom fusion | flops 262144 | bytes 4719104 | tf_op jit(solution)/shard_map/scatter-add | solution.py:375
  323.9 10.2 %all-to-all-done.3.coeff_ref = bf16[4,64,32,96]{3,2,1,0:T(8,128)(2,1)S(1)} async-done(((bf16[4,64,32,96]{3,2,1,0:T(8,128)(2,1)}), bf16[4,64,32,96]{3,2,1,0:T(8,128)(2,1)S(1)}, u32[]{:S(2)}, u32[]{:S(2)}) %all-to-all-start.3) | async-done | bytes 1572896 | tf_op jit(solution)/shard_map/all_to_all | solution.py:393
  334.1 1.3 copy-done.4
  335.4 3.4 copy-done.3
  338.8 1.6 copy-done.5
  340.4 6.5 %shard_map.116 = f32[64,32,256]{2,1,0:T(8,128)S(1)} custom-call(bf16[4,64,32,96]{3,2,1,0:T(8,128)(2,1)S(1)} %copy-done.5, bf16[64,256,256]{2,1,0:T(8,128)(2,1)S(1)} %copy-done.3), custom_call_target="tpu_custom_call" | custom-call | tf_op jit(solution)/shard_map/pallas_call | solution.py:190
  346.9 2.5 copy.111
  (77 shorter events, 9.1 us)
Async XLA Ops:
  0.6 127.9 %copy-start = (bf16[96,96,128]{2,1,0:T(8,128)(2,1)S(1)}, bf16[96,96,128]{2,1,0:T(8,128)(2,1)}, u32[]{:S(2)}) copy-start(bf16[96,96,128]{2,1,0:T(8,128)(2,1)} %param.11) | copy-start | bytes 7077892
  4.7 37.4 %copy-start.9 = (s32[1,2048]{1,0:T(1,128)S(1)}, s32[1,2048]{1,0:T(1,128)}, u32[]{:S(2)}) copy-start(s32[1,2048]{1,0:T(1,128)} %param.12) | copy-start | bytes 24580
  4.7 70.5 %copy-start.16 = (u32[32]{0:T(128)S(1)}, u32[32]{0:T(128)}, u32[]{:S(2)}) copy-start(u32[32]{0:T(128)} %constant.156) | copy-start | bytes 388
  32.9 3.2 copy-start.2
  36.2 1.3 copy-start.6
  37.5 54.0 %all-to-all-start = ((bf16[4,64,32,96]{3,2,1,0:T(8,128)(2,1)}), bf16[4,64,32,96]{3,2,1,0:T(8,128)(2,1)}, u32[]{:S(2)}, u32[]{:S(2)}) async-start(bf16[4,64,32,96]{3,2,1,0:T(8,128)(2,1)} %copy-done.6), calls=%async_computation | async-start | bytes 4194304 | tf_op jit(solution)/shard_map/all_to_all | solution.py:339
  87.5 11.0 %copy-start.11 = (f32[256]{0:T(256)}, f32[256]{0:T(256)S(1)}, u32[]{:S(2)}) copy-start(f32[256]{0:T(256)S(1)} %get-tuple-element.21) | copy-start | bytes 3076
  101.3 26.7 %copy-start.10 = (s32[2048,1]{0,1:T(1,128)S(1)}, s32[2048,1]{0,1:T(1,128)}, u32[]{:S(2)}) copy-start(s32[2048,1]{0,1:T(1,128)} %compare_select_fusion) | copy-start | bytes 24580
  124.3 13.9 %all-to-all-start.1 = ((bf16[8,16,2048]{2,1,0:T(8,128)(2,1)}), bf16[8,16,2048]{2,1,0:T(8,128)(2,1)S(1)}, u32[]{:S(2)}, u32[]{:S(2)}) async-start(bf16[8,16,2048]{2,1,0:T(8,128)(2,1)} %shard_map.114), calls=%async_computation.1 | async-start | bytes 1048576 | tf_op jit(solution)/shard_map/all_to_all | solution.py:363
  138.6 2.4 copy-start.13
  141.1 6.8 %copy-start.7 = (f32[2048,1024]{1,0:T(8,128)}, f32[2048,1024]{1,0:T(8,128)S(1)}, u32[]{:S(2)}) copy-start(f32[2048,1024]{1,0:T(8,128)S(1)} %fusion.45) | copy-start | bytes 25165828
  141.1 6.8 %copy-start.14 = (bf16[1024,512]{1,0:T(8,128)(2,1)S(1)}, bf16[1024,512]{1,0:T(8,128)(2,1)}, u32[]{:S(2)}) copy-start(bf16[1024,512]{1,0:T(8,128)(2,1)} %param.19) | copy-start | bytes 3145732
  141.1 6.8 %copy-start.15 = (f32[512]{0:T(512)S(1)}, f32[512]{0:T(512)}, u32[]{:S(2)}) copy-start(f32[512]{0:T(512)} %param.16) | copy-start | bytes 6148
  147.9 13.7 %copy-start.8 = (bf16[128,1024]{1,0:T(8,128)(2,1)S(1)}, bf16[128,1024]{1,0:T(8,128)(2,1)}, u32[]{:S(2)}) copy-start(bf16[128,1024]{1,0:T(8,128)(2,1)} %param.17) | copy-start | bytes 786436
  161.6 17.1 %copy-start.12 = (f32[256]{0:T(256)S(1)}, f32[256]{0:T(256)}, u32[]{:S(2)}) copy-start(f32[256]{0:T(256)} %copy-done.11) | copy-start | bytes 3076
  174.4 14.5 %all-to-all-start.2 = ((bf16[8,16,2048]{2,1,0:T(8,128)(2,1)}), bf16[8,16,2048]{2,1,0:T(8,128)(2,1)S(1)}, u32[]{:S(2)}, u32[]{:S(2)}) async-start(bf16[8,16,2048]{2,1,0:T(8,128)(2,1)} %bitcast.28), calls=%async_computation.2 | async-start | bytes 1048576 | tf_op jit(solution)/shard_map/all_to_all | solution.py:379
  304.8 29.3 %all-to-all-start.3 = ((bf16[4,64,32,96]{3,2,1,0:T(8,128)(2,1)}), bf16[4,64,32,96]{3,2,1,0:T(8,128)(2,1)S(1)}, u32[]{:S(2)}, u32[]{:S(2)}) async-start(bf16[4,64,32,96]{3,2,1,0:T(8,128)(2,1)} %bitcast.139), calls=%async_computation.3 | async-start | bytes 4194304 | tf_op jit(solution)/shard_map/all_to_all | solution.py:393
  334.1 1.3 copy-start.4
  335.4 3.4 copy-start.3
  338.8 1.6 copy-start.5
  340.4 9.1 %copy-start.1 = (bf16[96,96,128]{2,1,0:T(8,128)(2,1)S(1)}, bf16[96,96,128]{2,1,0:T(8,128)(2,1)}, u32[]{:S(2)}) copy-start(bf16[96,96,128]{2,1,0:T(8,128)(2,1)} %param.11) | copy-start | bytes 7077892

commit v3 on v2

--- a/solution.py
+++ b/solution.py
@@ -243,20 +243,22 @@
         sums[o][...] = jnp.zeros(sums[o].shape, jnp.float32)
         most = jnp.maximum(most, count_ref[o])
 
-    def one(slot, carry):
-        base = pl.multiple_of((slot // HALF) * HALF, HALF)
-        spot = slot % HALF
-        for o in range(owners):
-            row = row_ref[o * capacity + slot]
-            to = lane_ref[o * capacity + slot]
-            values = values_ref[o, :, pl.ds(base, HALF)]
-            moved = pltpu.roll(values, (to - spot + HALF) % HALF, 1)
-            sums[o][row] = sums[o][row] + jnp.where(lane == to, moved, 0.0)
-        return carry
-
     def several(group, carry):
+        terms = []
         for k in range(4):
-            one(group * 4 + k, carry)
+            slot = group * 4 + k
+            base = pl.multiple_of((slot // HALF) * HALF, HALF)
+            spot = slot % HALF
+            for o in range(owners):
+                to = lane_ref[o * capacity + slot]
+                values = values_ref[o, :, pl.ds(base, HALF)]
+                moved = pltpu.roll(values, (to - spot) & (HALF - 1), 1)
+                terms.append(jnp.where(lane == to, moved, 0.0))
+        for k in range(4):
+            rows = [row_ref[o * capacity + group * 4 + k] for o in range(owners)]
+            added = [sums[o][rows[o]] + terms[k * owners + o] for o in range(owners)]
+            for o in range(owners):
+                sums[o][rows[o]] = added[o]
         return carry
 
     lax.fori_loop(0, (most + 3) // 4, several, 0)
@@ -344,8 +346,10 @@
     local_cols = columns[0]
     owners = all_levels // levels
     capacity = local_cols.shape[0]
-    listed = lax.all_gather(local_cols, "lev")
-    band_counts = lax.all_gather(counts, "lev", tiled=True)
+    listed = jnp.concatenate([local_cols, jnp.broadcast_to(counts, (HALF,))])
+    listed = lax.all_gather(listed, "lev")
+    band_counts = listed[:, capacity]
+    listed = listed[:, :capacity]
     tiles = NLON // HALF
     list_rows = listed // tile_cols
     list_lanes = listed % tile_cols

time: 351 us -> 309 us (0.88)
  Pallas kernels: 169 us -> 136 us
  blocking collectives: 43.1 us -> 32.3 us
  starting transfers between devices: 16.3 us -> 20.7 us
    pallas_call x1, Pallas kernels: 111 us -> 78.6 us  [spread(): pl.pallas_call(spread_kernel, grid_spec=pltpu.PrefetchScalarGridSpec(num_...]
    unnamed x1 -> x0, blocking collectives: 10.8 us -> none
    unnamed x41 -> x38, local copies, waits for them, and re-layouts: 12.3 us -> 11 us
  transfers between devices with their start and end apart: 4 -> 4, of which waited for: 3 -> 3; matrix products, arithmetic and copies ran while one was open for 10% -> 11% of each run, Pallas kernels for 0% -> 0%
where the time goes in v3:
time: 309 us; the launch traced here: 310 us
  Pallas kernels  136 us (44%)
  matrix products  40.3 us (13%)
  local copies, waits for them, and re-layouts  33.3 us (11%)
  blocking collectives  32.3 us (10%)
  other arithmetic  27.3 us (9%)
  starting transfers between devices  20.7 us (7%)
  waiting for transfers between devices  18 us (6%)
    pallas_call x1, Pallas kernels, spread(): pl.pallas_call(spread_kernel, grid_spec=pltpu.PrefetchScalarGridSpec(num_...  78.6 us
    all_gather x1, blocking collectives, per_device(): listed = lax.all_gather(listed, 'lev')  32.3 us
    pallas_call x1, Pallas kernels, synthesis(): pl.pallas_call(functools.partial(synthesis_kernel, half_lats), grid=(wave...  28.1 us
    pallas_call x1, Pallas kernels, pick(): pl.pallas_call(pick_kernel, grid_spec=pltpu.PrefetchScalarGridSpec(num_sc...  22.7 us
    scatter-add x1, other arithmetic, per_device(): jnp.zeros(cell_rows.shape, jnp.float32).at[local_cols]  14 us
    dot_general x1, matrix products, radiance_pass(): jnp.dot(misfit, weight_out.T, preferred_element_type=jnp.float32)  13.7 us
    dot_general x1, matrix products, radiance_pass(): jnp.dot(back_first, weight_in.T, preferred_element_type=jnp.float32)  12.8 us
    unnamed x38, local copies, waits for them, and re-layouts  11 us
  transfers between devices with their start and end apart: 4, of which 3 were waited for; matrix products, arithmetic and copies ran while one was open for 11% of the time, Pallas kernels for 0%

profile of v3, /device:TPU:0, one launch (start us, length us, event | category | flops | bytes accessed | tf_op | source)
XLA Modules:
  0.0 309.5 jit_solution(17846920590590442098)
XLA Ops:
  1.5 1.7 convert_bitcast_fusion
  4.7 28.1 %shard_map.113 = (bf16[64,256,256]{2,1,0:T(8,128)(2,1)S(1)}, bf16[4,64,32,96]{3,2,1,0:T(8,128)(2,1)S(1)}) custom-call(f32[32,64,8]{2,1,0:T(8,128)S(1)} %get-tuple-element.12.fa_ref, f32[32,64,8]{2,1,0:T(8,128)S(1)} %get-tuple-element.11.fb_ref, f32[64,256]{1,0:T(8,128)S(1)} %pad.17.log_ref, f32[1,256]{1,0:T(1,128)S(1)} %bitcast.101, f32[1,256]{1,0:T(1,128)S(1)} %bitcast.102, ...), custom_call_target="tpu_custom_call" | custom-call | tf_op jit(solution)/shard_map/pallas_call | solution.py:161
  32.9 3.2 %copy-done.2 = bf16[64,256,256]{2,1,0:T(8,128)(2,1)} copy-done((bf16[64,256,256]{2,1,0:T(8,128)(2,1)}, bf16[64,256,256]{2,1,0:T(8,128)(2,1)S(1)}, u32[]{:S(2)}) %copy-start.2) | copy-done | bytes 8388632
  36.1 1.3 copy-done.6
  37.5 4.5 %all-to-all-start = ((bf16[4,64,32,96]{3,2,1,0:T(8,128)(2,1)}), bf16[4,64,32,96]{3,2,1,0:T(8,128)(2,1)}, u32[]{:S(2)}, u32[]{:S(2)}) async-start(bf16[4,64,32,96]{3,2,1,0:T(8,128)(2,1)} %copy-done.6), calls=%async_computation | async-start | bytes 4194304 | tf_op jit(solution)/shard_map/all_to_all | solution.py:341
  42.7 32.3 %all-gather.1 = s32[8,1,2176]{2,1,0:T(1,128)S(1)} all-gather(s32[1,1,2176]{2,1,0:T(1,128)S(1)} %reshape.396), channel_id=2, replica_groups=mesh['lat'=4,'lev'=8] {'lev'}, dimensions={0}, use_global_device_ids=true | all-gather | bytes 78336 | tf_op jit(solution)/shard_map/all_gather | solution.py:350
  75.4 3.4 %multiply_convert_fusion.13 = (bf16[1,256,6,128]{3,1,0,2:T(8,128)(2,1)S(1)}, bf16[1,256,6,128]{3,1,0,2:T(8,128)(2,1)S(1)}) fusion(s32[6,128]{1,0:T(8,128)S(1)} %multiply_add_fusion.2, f32[256]{0:T(256)S(1)} %get-tuple-element.21, f32[256]{0:T(256)S(1)} %get-tuple-element.22), kind=kLoop, calls=%fused_computation.61 | loop fusion | flops 2555904 | bytes 791552 | tf_op jit(solution)/shard_map/convert.3
  79.4 4.2 %copy.58 = bf16[256,2,16,96]{0,3,1,2:T(8,128)(2,1)} copy(bf16[256,2,16,96]{3,2,1,0:T(8,128)(2,1)} %bitcast.14) | data formatting | bytes 3145728 | tf_op jit(solution)/shard_map/reshape | solution.py:343
  83.6 2.8 convolution_bitcast_fusion
  86.4 2.7 copy.59
  89.2 22.7 %shard_map.114 = bf16[8,16,2048]{2,1,0:T(8,128)(2,1)} custom-call(s32[16384]{0:T(1024)S(1)} %bitcast.97, s32[16384]{0:T(1024)S(1)} %bitcast.98, s32[8]{0:T(128)S(1)} %slice_reduce_fusion.count_ref, f32[576,16,128]{2,1,0:T(8,128)S(1)} %bitcast.94), custom_call_target="tpu_custom_call" | custom-call | tf_op jit(solution)/shard_map/pallas_call | solution.py:225
  111.9 5.5 %all-to-all-start.1 = ((bf16[8,16,2048]{2,1,0:T(8,128)(2,1)}), bf16[8,16,2048]{2,1,0:T(8,128)(2,1)S(1)}, u32[]{:S(2)}, u32[]{:S(2)}) async-start(bf16[8,16,2048]{2,1,0:T(8,128)(2,1)} %shard_map.114), calls=%async_computation.1 | async-start | bytes 1048576 | tf_op jit(solution)/shard_map/all_to_all | solution.py:367
  118.0 7.2 %gather_fusion = bf16[2048,128]{1,0:T(8,128)(2,1)S(1)} fusion(bf16[9216,128]{1,0:T(8,128)(2,1)S(1)} %bitcast.93, s32[2048]{0:T(1024)} %broadcast_clamp_fusion), kind=kCustom, calls=%fused_computation | custom fusion | bytes 1056768 | tf_op jit(solution)/shard_map/jit(_take)/gather | solution.py:370
  125.9 1.8 all-to-all-done.1
  128.2 2.4 fusion.45
  130.6 6.8 %fusion.3 = f32[2048,1024]{1,0:T(8,128)} fusion(bf16[1024,1024]{1,0:T(8,128)(2,1)S(1)} %copy-done.13, f32[2048,1024]{1,0:T(8,128)S(1)} %fusion.45), kind=kOutput, calls=%fused_computation.13 | convolution fusion | flops 4305453056 | bytes 18874368 | tf_op jit(solution)/shard_map/dot_general | solution.py:306
  137.4 13.7 %multiply_convert_fusion.1 = bf16[2048,1024]{1,0:T(8,128)(2,1)} fusion(f32[2048,1024]{1,0:T(8,128)} %fusion.3, bf16[1024,512]{1,0:T(8,128)(2,1)S(1)} %copy-done.14, bf16[1,2048,512]{2,1,0:T(8,128)(2,1)} %param.14, f32[512]{0:T(512)S(1)} %copy-done.15, f32[2048]{0:T(1024)S(1)} %bitcast.113, pred[2048]{0:T(1024)(128)(4,1)S(1)} %iota_compare_fusion.2), kind=kOutput, calls=%fused_computation.3 | convolution fusion | flops 4331667456 | bytes 15740928 | tf_op jit(solution)/shard_map/dot_general | solution.py:315
  151.2 12.8 %convolution_convert_fusion = bf16[2048,128]{0,1:T(8,128)(2,1)} fusion(bf16[128,1024]{1,0:T(8,128)(2,1)S(1)} %copy-done.8, f32[2048,1024]{1,0:T(8,128)} %copy-done.7, bf16[2048,1024]{1,0:T(8,128)(2,1)} %multiply_convert_fusion.1, bf16[1024,1024]{1,0:T(8,128)(2,1)} %param.18), kind=kOutput, calls=%fused_computation.20 | convolution fusion | flops 4850974720 | bytes 15466496 | tf_op jit(solution)/shard_map/dot_general | solution.py:321
  163.9 4.2 %all-to-all-start.2 = ((bf16[8,16,2048]{2,1,0:T(8,128)(2,1)}), bf16[8,16,2048]{2,1,0:T(8,128)(2,1)S(1)}, u32[]{:S(2)}, u32[]{:S(2)}) async-start(bf16[8,16,2048]{2,1,0:T(8,128)(2,1)} %bitcast.24), calls=%async_computation.2 | async-start | bytes 1048576 | tf_op jit(solution)/shard_map/all_to_all | solution.py:383
  168.2 4.5 %multiply_convert_fusion.11 = (bf16[1,256,8,96]{3,1,2,0:T(8,128)(2,1)S(1)}, bf16[1,256,8,96]{3,1,2,0:T(8,128)(2,1)S(1)}) fusion(s32[8,96]{1,0:T(8,128)S(1)} %multiply_add_fusion.3, f32[256]{0:T(256)S(1)} %get-tuple-element.21, f32[256]{0:T(256)S(1)} %copy-done.12), kind=kLoop, calls=%fused_computation.50 | loop fusion | flops 2555904 | bytes 791552 | tf_op jit(solution)/shard_map/convert.5
  172.7 5.7 %all-to-all-done.2 = bf16[8,16,2048]{2,1,0:T(8,128)(2,1)S(1)} async-done(((bf16[8,16,2048]{2,1,0:T(8,128)(2,1)}), bf16[8,16,2048]{2,1,0:T(8,128)(2,1)S(1)}, u32[]{:S(2)}, u32[]{:S(2)}) %all-to-all-start.2) | async-done | bytes 524320 | tf_op jit(solution)/shard_map/all_to_all | solution.py:383
  178.5 78.6 %shard_map.115 = bf16[8,96,16,128]{3,2,1,0:T(8,128)(2,1)S(1)} custom-call(s32[16384]{0:T(1024)S(1)} %bitcast.99, s32[16384]{0:T(1024)S(1)} %bitcast.100, s32[8]{0:T(128)S(1)} %slice_reduce_fusion.count_ref, f32[8,16,2048]{2,1,0:T(8,128)S(1)} %convert_element_type.135.values_ref), custom_call_target="tpu_custom_call" | custom-call | tf_op jit(solution)/shard_map/pallas_call | solution.py:272
  257.1 1.9 fusion.22
  259.0 3.0 copy.62
  262.0 6.5 %all-to-all-start.3 = ((bf16[4,64,32,96]{3,2,1,0:T(8,128)(2,1)}), bf16[4,64,32,96]{3,2,1,0:T(8,128)(2,1)S(1)}, u32[]{:S(2)}, u32[]{:S(2)}) async-start(bf16[4,64,32,96]{3,2,1,0:T(8,128)(2,1)} %bitcast.103), calls=%async_computation.3 | async-start | bytes 4194304 | tf_op jit(solution)/shard_map/all_to_all | solution.py:397
  269.7 14.0 %scatter_custom_fusion = f32[9216,128]{1,0:T(8,128)} fusion(s32[2048]{0:T(1024)} %bitcast.111, f32[2048,128]{1,0:T(8,128)S(1)} %copy.64, f32[]{:T(128)} %constant.137.clone.1), kind=kCustom, calls=%fused_computation.21 | custom fusion | flops 262144 | bytes 4719104 | tf_op jit(solution)/shard_map/scatter-add | solution.py:379
  283.8 10.4 %all-to-all-done.3.coeff_ref = bf16[4,64,32,96]{3,2,1,0:T(8,128)(2,1)S(1)} async-done(((bf16[4,64,32,96]{3,2,1,0:T(8,128)(2,1)}), bf16[4,64,32,96]{3,2,1,0:T(8,128)(2,1)S(1)}, u32[]{:S(2)}, u32[]{:S(2)}) %all-to-all-start.3) | async-done | bytes 1572896 | tf_op jit(solution)/shard_map/all_to_all | solution.py:397
  294.2 1.3 copy-done.4
  295.5 3.4 %copy-done.3 = bf16[64,256,256]{2,1,0:T(8,128)(2,1)S(1)} copy-done((bf16[64,256,256]{2,1,0:T(8,128)(2,1)S(1)}, bf16[64,256,256]{2,1,0:T(8,128)(2,1)}, u32[]{:S(2)}) %copy-start.3) | copy-done | bytes 8388632
  298.9 1.6 copy-done.5
  300.5 6.5 %shard_map.116 = f32[64,32,256]{2,1,0:T(8,128)S(1)} custom-call(bf16[4,64,32,96]{3,2,1,0:T(8,128)(2,1)S(1)} %copy-done.5, bf16[64,256,256]{2,1,0:T(8,128)(2,1)S(1)} %copy-done.3), custom_call_target="tpu_custom_call" | custom-call | tf_op jit(solution)/shard_map/pallas_call | solution.py:190
  307.0 2.5 copy.84
  (75 shorter events, 6.5 us)
Async XLA Ops:
  0.6 117.4 %copy-start = (bf16[96,96,128]{2,1,0:T(8,128)(2,1)S(1)}, bf16[96,96,128]{2,1,0:T(8,128)(2,1)}, u32[]{:S(2)}) copy-start(bf16[96,96,128]{2,1,0:T(8,128)(2,1)} %param.11) | copy-start | bytes 7077892
  4.7 38.0 %copy-start.9 = (s32[1,2048]{1,0:T(1,128)S(1)}, s32[1,2048]{1,0:T(1,128)}, u32[]{:S(2)}) copy-start(s32[1,2048]{1,0:T(1,128)} %param.12) | copy-start | bytes 24580
  32.9 3.2 %copy-start.2 = (bf16[64,256,256]{2,1,0:T(8,128)(2,1)}, bf16[64,256,256]{2,1,0:T(8,128)(2,1)S(1)}, u32[]{:S(2)}) copy-start(bf16[64,256,256]{2,1,0:T(8,128)(2,1)S(1)} %get-tuple-element.5.table_ref) | copy-start | bytes 25165828
  36.1 1.3 copy-start.6
  37.5 42.0 %all-to-all-start = ((bf16[4,64,32,96]{3,2,1,0:T(8,128)(2,1)}), bf16[4,64,32,96]{3,2,1,0:T(8,128)(2,1)}, u32[]{:S(2)}, u32[]{:S(2)}) async-start(bf16[4,64,32,96]{3,2,1,0:T(8,128)(2,1)} %copy-done.6), calls=%async_computation | async-start | bytes 4194304 | tf_op jit(solution)/shard_map/all_to_all | solution.py:341
  75.3 11.1 %copy-start.11 = (f32[256]{0:T(256)}, f32[256]{0:T(256)S(1)}, u32[]{:S(2)}) copy-start(f32[256]{0:T(256)S(1)} %get-tuple-element.22) | copy-start | bytes 3076
  89.2 28.2 %copy-start.10 = (s32[2048,1]{0,1:T(1,128)S(1)}, s32[2048,1]{0,1:T(1,128)}, u32[]{:S(2)}) copy-start(s32[2048,1]{0,1:T(1,128)} %compare_select_fusion) | copy-start | bytes 24580
  111.9 15.8 %all-to-all-start.1 = ((bf16[8,16,2048]{2,1,0:T(8,128)(2,1)}), bf16[8,16,2048]{2,1,0:T(8,128)(2,1)S(1)}, u32[]{:S(2)}, u32[]{:S(2)}) async-start(bf16[8,16,2048]{2,1,0:T(8,128)(2,1)} %shard_map.114), calls=%async_computation.1 | async-start | bytes 1048576 | tf_op jit(solution)/shard_map/all_to_all | solution.py:367
  128.2 2.4 copy-start.13
  130.6 6.8 %copy-start.7 = (f32[2048,1024]{1,0:T(8,128)}, f32[2048,1024]{1,0:T(8,128)S(1)}, u32[]{:S(2)}) copy-start(f32[2048,1024]{1,0:T(8,128)S(1)} %fusion.45) | copy-start | bytes 25165828
  130.6 6.8 %copy-start.14 = (bf16[1024,512]{1,0:T(8,128)(2,1)S(1)}, bf16[1024,512]{1,0:T(8,128)(2,1)}, u32[]{:S(2)}) copy-start(bf16[1024,512]{1,0:T(8,128)(2,1)} %param.19) | copy-start | bytes 3145732
  130.6 6.8 %copy-start.15 = (f32[512]{0:T(512)S(1)}, f32[512]{0:T(512)}, u32[]{:S(2)}) copy-start(f32[512]{0:T(512)} %param.16) | copy-start | bytes 6148
  137.4 13.7 %copy-start.8 = (bf16[128,1024]{1,0:T(8,128)(2,1)S(1)}, bf16[128,1024]{1,0:T(8,128)(2,1)}, u32[]{:S(2)}) copy-start(bf16[128,1024]{1,0:T(8,128)(2,1)} %param.17) | copy-start | bytes 786436
  151.2 17.0 %copy-start.12 = (f32[256]{0:T(256)S(1)}, f32[256]{0:T(256)}, u32[]{:S(2)}) copy-start(f32[256]{0:T(256)} %copy-done.11) | copy-start | bytes 3076
  163.9 14.5 %all-to-all-start.2 = ((bf16[8,16,2048]{2,1,0:T(8,128)(2,1)}), bf16[8,16,2048]{2,1,0:T(8,128)(2,1)S(1)}, u32[]{:S(2)}, u32[]{:S(2)}) async-start(bf16[8,16,2048]{2,1,0:T(8,128)(2,1)} %bitcast.24), calls=%async_computation.2 | async-start | bytes 1048576 | tf_op jit(solution)/shard_map/all_to_all | solution.py:383
  262.0 32.2 %all-to-all-start.3 = ((bf16[4,64,32,96]{3,2,1,0:T(8,128)(2,1)}), bf16[4,64,32,96]{3,2,1,0:T(8,128)(2,1)S(1)}, u32[]{:S(2)}, u32[]{:S(2)}) async-start(bf16[4,64,32,96]{3,2,1,0:T(8,128)(2,1)} %bitcast.103), calls=%async_computation.3 | async-start | bytes 4194304 | tf_op jit(solution)/shard_map/all_to_all | solution.py:397
  294.2 1.3 copy-start.4
  295.5 3.4 %copy-start.3 = (bf16[64,256,256]{2,1,0:T(8,128)(2,1)S(1)}, bf16[64,256,256]{2,1,0:T(8,128)(2,1)}, u32[]{:S(2)}) copy-start(bf16[64,256,256]{2,1,0:T(8,128)(2,1)} %copy-done.2) | copy-start | bytes 25165828
  298.9 1.6 copy-start.5
  300.5 9.1 %copy-start.1 = (bf16[96,96,128]{2,1,0:T(8,128)(2,1)S(1)}, bf16[96,96,128]{2,1,0:T(8,128)(2,1)}, u32[]{:S(2)}) copy-start(bf16[96,96,128]{2,1,0:T(8,128)(2,1)} %param.11) | copy-start | bytes 7077892
